TPU v7x, 32 devices: a whole 2x2x4 slice. The times are simulated.
32 devices in a mesh: section: 2 (over x), lat: 4 (over z), tp: 4 (over y, core).
Axes of the slice: x: 2, y: 2, z: 4, core: 2. Of those that a mesh axis runs over, the one named last changes fastest.
Arguments:
- initial_field: bfloat16 [2, 8, 12, 48, 192], P(None, 'tp', 'lat'), may hold values from -6 to 6
- first_gain: bfloat16 [2, 192], P('section'), may hold values from 0.25 to 1.75
- first_shift: bfloat16 [2, 192], P('section'), may hold values from -1.75 to 1.75
- qkv_weight: bfloat16 [2, 192, 576], P('section', None, 'tp'), may hold values from -0.4375 to 0.4375
- qkv_bias: bfloat16 [2, 576], P('section', 'tp'), may hold values from -1.75 to 1.75
- proj_weight: bfloat16 [2, 192, 192], P('section', None, 'tp'), may hold values from -0.4375 to 0.4375
- proj_bias: bfloat16 [2, 192], P('section', 'tp'), may hold values from -1.75 to 1.75
- second_gain: bfloat16 [2, 192], P('section'), may hold values from 0.25 to 1.75
- second_shift: bfloat16 [2, 192], P('section'), may hold values from -1.75 to 1.75
- expand_weight: bfloat16 [2, 192, 768], P('section', None, 'tp'), may hold values from -0.4375 to 0.4375
- expand_bias: bfloat16 [2, 768], P('section', 'tp'), may hold values from -1.75 to 1.75
- reduce_weight: bfloat16 [2, 768, 192], P('section', 'tp'), may hold values from -0.21875 to 0.21875
- reduce_bias: bfloat16 [2, 192], P('section', 'tp'), may hold values from -1.75 to 1.75
- earth_bias: float32 [2, 4, 4, 6, 1656], P('section', 'tp', 'lat'), may hold values from -4 to 340
Outputs:
- predicted_states: bfloat16 [2, 2, 8, 12, 48, 192], P('section', None, 'tp', 'lat')
All inputs are finite; a program needn't handle non-finite values.
Results may differ from a plain program's by a relative error of at most 0.018.
Values may be sent and summed in bfloat16 or wider, within the bound.
A program may use at most 64 MiB of HBM per device.

v0:
```python
import jax
import jax.numpy as jnp
import numpy as np
from jax import lax
from jax.sharding import PartitionSpec as P

WZ = 2
WH = 6
WW = 12


epsilon = 1e-05


def swapped(block, axis, apart):
    count = lax.axis_size(axis)
    route = []
    for low in range(count):
        high = low | 1 << apart
        if high != low and high < count:
            route += [(low, high), (high, low)]
    return lax.ppermute(block, axis, route)


def passed_along(value, axis, steps):
    count = lax.axis_size(axis)
    first, last = (max(0, -steps), min(count, count - steps))
    return lax.ppermute(value, axis, [(source, source + steps) for source in range(first, last)])


def bias_entries():
    half_rows = WH // 2
    query_pos = np.arange(WZ * half_rows * WW)
    attended_location = np.arange(WZ * WH * WW)
    query_level = query_pos // (half_rows * WW)
    query_row = query_pos // WW % half_rows
    query_col = query_pos % WW
    key_level = attended_location // (WH * WW)
    key_row = attended_location // WW % WH
    key_column_index = attended_location % WW
    table_items = (
        ((query_level[:, None] * WZ + key_level[None, :]) * half_rows + query_row[:, None]) * WH
        + key_row[None, :]
    ) * (2 * WW - 1) + (query_col[:, None] - key_column_index[None, :] + WW - 1)
    return table_items.astype(np.int32)


def layer_norm(values, gain, offset):
    floats = values.astype(jnp.float32)
    middle_point = jnp.mean(floats, axis=-1, keepdims=True)
    spread = jnp.mean((floats - middle_point) ** 2, axis=-1, keepdims=True)
    return (floats - middle_point) * lax.rsqrt(spread + epsilon) * gain.astype(
        jnp.float32
    ) + offset.astype(jnp.float32)


def earth_block(grid, norms, weights, bias_block, band_half):
    first_gain, first_shift, second_gain, second_shift = norms
    (
        qkv_matrix,
        qkv_offset,
        proj_matrix,
        proj_offset,
        expand_matrix,
        expand_offset,
        reduce_matrix,
        shrink_translation,
    ) = weights
    levels, lat_rows, lon_cols, width = grid.shape
    heads = bias_block.shape[0]
    head_size = width // heads
    scale = 1.0 / float(np.sqrt(head_size))
    meridian_slabs = lon_cols // WW
    normed = layer_norm(grid, first_gain, first_shift).astype(jnp.bfloat16)
    flat = normed.reshape(-1, width)
    own_mixed = (
        jnp.dot(flat, qkv_matrix, preferred_element_type=jnp.float32)
        + qkv_offset.astype(jnp.float32)
    ).astype(jnp.bfloat16)
    neighbour_keyvalue = swapped(own_mixed[:, width:], "lat", 0)
    own_kv = own_mixed[:, width:].reshape(levels, lat_rows, lon_cols, 2 * width)
    neighbour_keyvalue = neighbour_keyvalue.reshape(levels, lat_rows, lon_cols, 2 * width)
    lower_first = jnp.concatenate([own_kv, neighbour_keyvalue], axis=1)
    upper_first = jnp.concatenate([neighbour_keyvalue, own_kv], axis=1)
    window_kv = jnp.where(band_half == 0, lower_first, upper_first)
    keyvals = window_kv.reshape(levels, 2 * lat_rows, meridian_slabs, WW, 2 * width).transpose(
        2, 0, 1, 3, 4
    )
    keyvals = keyvals.reshape(meridian_slabs, levels * 2 * lat_rows * WW, 2 * width)
    query_rows = (
        own_mixed[:, :width]
        .reshape(levels, lat_rows, meridian_slabs, WW, width)
        .transpose(2, 0, 1, 3, 4)
    )
    query_rows = query_rows.reshape(meridian_slabs, levels * lat_rows * WW, width)
    query_count = query_rows.shape[1]
    key_count = keyvals.shape[1]
    query_heads = query_rows.reshape(meridian_slabs, query_count, heads, head_size)
    key_heads = keyvals[..., :width].reshape(meridian_slabs, key_count, heads, head_size)
    value_heads = keyvals[..., width:].reshape(meridian_slabs, key_count, heads, head_size)
    scores = (
        jnp.einsum("wqhd,wkhd->whqk", query_heads, key_heads, preferred_element_type=jnp.float32)
        * scale
        + bias_block[None]
    )
    probs = jax.nn.softmax(scores, axis=-1).astype(jnp.bfloat16)
    attended = jnp.einsum(
        "whqk,wkhd->wqhd", probs, value_heads, preferred_element_type=jnp.float32
    ).astype(jnp.bfloat16)
    merged = (
        attended.reshape(meridian_slabs, levels, lat_rows, WW, width)
        .transpose(1, 2, 0, 3, 4)
        .reshape(-1, width)
    )
    branch = jnp.dot(merged, proj_matrix, preferred_element_type=jnp.float32) + proj_offset.astype(
        jnp.float32
    )
    middle = (grid.reshape(-1, width).astype(jnp.float32) + branch).astype(jnp.bfloat16)
    normed_two = layer_norm(middle, second_gain, second_shift).astype(jnp.bfloat16)
    hidden = jax.nn.gelu(
        jnp.dot(normed_two, expand_matrix, preferred_element_type=jnp.float32)
        + expand_offset.astype(jnp.float32),
        approximate=False,
    ).astype(jnp.bfloat16)
    result = (
        middle.astype(jnp.float32)
        + jnp.dot(hidden, reduce_matrix, preferred_element_type=jnp.float32)
        + shrink_translation.astype(jnp.float32)
    ).astype(jnp.bfloat16)
    return result.reshape(levels, lat_rows, lon_cols, width)


def on_device(
    initial_field,
    first_gain,
    first_shift,
    qkv_weight,
    qkv_bias,
    proj_weight,
    proj_bias,
    second_gain,
    second_shift,
    expand_weight,
    expand_bias,
    reduce_weight,
    reduce_bias,
    earth_bias,
):
    collected_values = (
        lax.all_gather(qkv_weight, "tp", axis=2, tiled=True),
        lax.all_gather(qkv_bias, "tp", axis=1, tiled=True),
        lax.all_gather(proj_weight, "tp", axis=2, tiled=True),
        lax.all_gather(proj_bias, "tp", axis=1, tiled=True),
        lax.all_gather(expand_weight, "tp", axis=2, tiled=True),
        lax.all_gather(expand_bias, "tp", axis=1, tiled=True),
        lax.all_gather(reduce_weight, "tp", axis=1, tiled=True),
        lax.all_gather(reduce_bias, "tp", axis=1, tiled=True),
    )
    weights = tuple((piece[0] for piece in collected_values))
    norms = (first_gain[0], first_shift[0], second_gain[0], second_shift[0])
    bias_table = earth_bias[0, 0, 0]
    table_items = jnp.asarray(bias_entries())
    portion_index = lax.axis_index("section")
    band_half = lax.axis_index("lat") % 2
    micro_count = initial_field.shape[0]
    bias_block = jnp.take(bias_table, table_items, axis=1)
    carried = jnp.zeros_like(initial_field[0])
    daily_lead_times = []
    quarter_lead_times = []
    for turn_index in range(micro_count + 1):
        own_field = initial_field[min(turn_index, micro_count - 1)]
        block_input = jnp.where(portion_index == 0, own_field, carried)
        block_output = earth_block(block_input, norms, weights, bias_block, band_half)
        if turn_index < micro_count:
            daily_lead_times.append(block_output)
            carried = passed_along(block_output, "section", 1)
        if turn_index > 0:
            quarter_lead_times.append(block_output)
    predicted_states = jnp.where(
        portion_index == 0, jnp.stack(daily_lead_times), jnp.stack(quarter_lead_times)
    )
    return predicted_states[None]


def solution(mesh):
    return jax.shard_map(
        on_device,
        mesh=mesh,
        in_specs=(
            P(None, "tp", "lat", None, None),
            P("section", None),
            P("section", None),
            P("section", None, "tp"),
            P("section", "tp"),
            P("section", None, "tp"),
            P("section", "tp"),
            P("section", None),
            P("section", None),
            P("section", None, "tp"),
            P("section", "tp"),
            P("section", "tp", None),
            P("section", "tp"),
            P("section", "tp", "lat", None, None),
        ),
        out_specs=P("section", None, "tp", "lat", None, None),
        check_vma=False,
    )
```

profile of v0, /device:TPU:0, one launch (start us, length us, event | category | flops | bytes accessed | tf_op | source)
XLA Modules:
  0.0 141.7 jit_solution(4354355133289032696)
XLA Ops:
  0.0 1.0 convert_reduce_fusion.4
  1.0 1.1 fusion.184
  3.5 1.2 dynamic-slice
  8.1 0.9 dynamic-update-slice.1
  10.2 8.5 %all-reduce.4 = (bf16[768]{0:T(1024)(128)(2,1)S(1)}, bf16[192]{0:T(256)(128)(2,1)S(1)}, bf16[576]{0:T(1024)(128)(2,1)S(1)}, bf16[192]{0:T(256)(128)(2,1)S(1)}) all-reduce(bf16[768]{0:T(1024)(128)(2,1)S(1)} %dynamic-update-slice.2, bf16[192]{0:T(256)(128)(2,1)S(1)} %dynamic-update-slice.1, ...), channel_id=1, replica_groups=mesh['section'=2,'lat'=4,'tp'=4] {'tp'}, use_global_device_ids=true, to_apply=%add.2 | all-reduce | flops 1728 | bytes 6912
  18.7 6.1 %all_gather.24 = bf16[1,192,576]{1,2,0:T(8,128)(2,1)S(1)} all-gather(bf16[1,192,144]{1,2,0:T(8,128)(2,1)} %param.18), channel_id=1, replica_groups=mesh['section'=2,'lat'=4,'tp'=4] {'tp'}, dimensions={2}, use_global_device_ids=true | all-gather | bytes 276480 | tf_op jit(solution)/shard_map/all_gather | solution.py:150
  24.8 1.1 add_convert_fusion.3
  26.4 1.6 %collective-permute-start = (bf16[288,384]{1,0:T(8,128)(2,1)S(1)}, bf16[288,384]{1,0:T(8,128)(2,1)}, u32[]{:S(2)}, u32[]{:S(2)}) collective-permute-start(bf16[288,384]{1,0:T(8,128)(2,1)S(1)} %slice.62), channel_id=1, source_target_pairs={{0,4},{4,0},{8,12},{12,8},{1,5},{5,1},{9,13},{13,9},{2,6},{6,2},{1... | collective-permute-start | bytes 663560 | tf_op jit(solution)/shard_map/ppermute | solution.py:22
  28.9 19.9 %gather_fusion = f32[10368,6]{1,0:T(8,128)} fusion(f32[6,1656]{0,1:T(8,128)S(1)} %bitcast.127, s32[11264]{0:T(1024)S(1)} %pad_clamp_fusion), kind=kCustom, calls=%fused_computation | custom fusion | bytes 539136 | tf_op jit(solution)/shard_map/jit(_take)/gather | solution.py:166
  48.8 4.8 %copy.74 = f32[72,144,6]{1,0,2:T(8,128)S(1)} copy(f32[72,144,6]{2,1,0:T(8,128)} %bitcast.128) | data formatting | bytes 497664 | tf_op jit(solution)/shard_map/jit(_take)/gather | solution.py:166
  53.7 5.5 %all_gather.26 = bf16[1,192,192]{1,2,0:T(8,128)(2,1)S(1)} all-gather(bf16[1,192,48]{1,2,0:T(8,128)(2,1)S(1)} %copy-done.10), channel_id=1, replica_groups=mesh['section'=2,'lat'=4,'tp'=4] {'tp'}, dimensions={2}, use_global_device_ids=true | all-gather | bytes 92160 | tf_op jit(solution)/shard_map/all_gather | solution.py:152
  60.5 8.7 %all_gather.28 = bf16[1,192,768]{1,0,2:T(2,128)(2,1)S(1)} all-gather(bf16[1,192,192]{1,0,2:T(2,128)(2,1)S(1)} %copy.77), channel_id=1, replica_groups=mesh['section'=2,'lat'=4,'tp'=4] {'tp'}, dimensions={2}, use_global_device_ids=true | all-gather | bytes 368640 | tf_op jit(solution)/shard_map/all_gather | solution.py:154
  69.7 7.8 %all_gather.30 = bf16[1,768,192]{2,1,0:T(8,128)(2,1)} all-gather(bf16[1,192,192]{2,1,0:T(8,128)(2,1)} %param.26), channel_id=1, replica_groups=mesh['section'=2,'lat'=4,'tp'=4] {'tp'}, dimensions={1}, use_global_device_ids=true | all-gather | bytes 368640 | tf_op jit(solution)/shard_map/all_gather | solution.py:156
  77.6 1.0 concatenate.51
  79.8 1.1 fusion.354
  80.9 3.8 %fusion.18 = bf16[4,72,6,32]{1,3,2,0:T(8,128)(2,1)} fusion(bf16[4,144,6,32]{1,3,2,0:T(8,128)(2,1)S(1)} %bitcast.155, f32[4,6,72]{2,1,0:T(8,128)S(1)} %fusion.354, f32[6,72,144]{2,1,0:T(8,128)S(1)} %bitcast.143, bf16[4,144,6,32]{1,3,2,0:T(8,128)(2,1)S(1)} %bitcast.151, bf16[4,72,6,32]{3,2,0,1:T(8,128)(2,1)S(1)} %reshape_reshape.9), kind=kOutput, calls=%fused_computation.46 | convolution fusion | flops 33151824 | bytes 919296 | tf_op jit(solution)/shard_map/whqk,wkhd->wqhd/dot_general | solution.py:107
  84.7 1.8 %copy.75 = bf16[4,72,6,32]{3,2,0,1:T(8,128)(2,1)S(1)} copy(bf16[4,72,6,32]{1,3,2,0:T(8,128)(2,1)} %fusion.18) | data formatting | bytes 221184 | tf_op jit(solution)/shard_map/convert_element_type | solution.py:109
  87.6 2.4 %fusion.17 = bf16[288,192]{1,0:T(8,128)(2,1)S(1)} fusion(f32[288,192]{1,0:T(8,128)S(1)} %get-tuple-element.20, f32[768]{0:T(1024)S(1)} %copy-done.11, bf16[1,768,192]{2,1,0:T(8,128)(2,1)S(1)} %copy-done.1, bf16[1,192,768]{2,1,0:T(8,128)(2,1)S(1)} %copy.78, f32[192]{0:T(256)S(1)} %copy-done.22, f32[192]{0:T(256)S(1)} %bitcast.171, f32[192]{0:T(256)S(1)} %bitcast.168, ...), kind=kOutput, calls=%fused_computation.45 | convolution fusion | flops 184909824 | bytes 929280 | tf_op jit(solution)/shard_map/dot_general | solution.py:127
  90.0 3.6 %collective-permute-start.1 = (bf16[2,3,48,192]{3,2,1,0:T(8,128)(2,1)S(1)}, bf16[2,3,48,192]{3,2,1,0:T(8,128)(2,1)S(1)}, u32[]{:S(2)}, u32[]{:S(2)}) collective-permute-start(bf16[2,3,48,192]{3,2,1,0:T(8,128)(2,1)S(1)} %bitcast.157), channel_id=1, source_target_pairs={{0,16},{1,17},{2,18},{3,19},{4,20},{5,21},{6,22},{7,23},{8,24},{9,... | collective-permute-start | bytes 331784 | tf_op jit(solution)/shard_map/ppermute | solution.py:28
  93.7 3.4 %collective-permute-done.1 = bf16[2,3,48,192]{3,2,1,0:T(8,128)(2,1)S(1)} collective-permute-done((bf16[2,3,48,192]{3,2,1,0:T(8,128)(2,1)S(1)}, bf16[2,3,48,192]{3,2,1,0:T(8,128)(2,1)S(1)}, u32[]{:S(2)}, u32[]{:S(2)}) %collective-permute-start.1) | collective-permute-done | bytes 110624 | tf_op jit(solution)/shard_map/ppermute | solution.py:28
  99.0 5.9 %collective-permute-done.2 = bf16[288,384]{1,0:T(8,128)(2,1)S(1)} collective-permute-done((bf16[288,384]{1,0:T(8,128)(2,1)S(1)}, bf16[288,384]{1,0:T(8,128)(2,1)S(1)}, u32[]{:S(2)}, u32[]{:S(2)}) %collective-permute-start.2) | collective-permute-done | bytes 221216 | tf_op jit(solution)/shard_map/ppermute | solution.py:22
  105.9 1.0 copy.80
  106.9 1.7 %fusion.358 = f32[4,6,72]{2,1,0:T(8,128)} fusion(f32[6,72,144]{2,1,0:T(8,128)S(1)} %bitcast.144, bf16[4,144,6,32]{1,3,2,0:T(8,128)(2,1)S(1)} %bitcast.152, bf16[4,72,6,32]{3,2,0,1:T(8,128)(2,1)S(1)} %reshape_reshape.10), kind=kOutput, calls=%fused_computation.393 | convolution fusion | flops 16920720 | bytes 587520 | tf_op jit(solution)/shard_map/sub | solution.py:106
  108.6 3.9 %fusion.19 = bf16[4,72,6,32]{1,3,2,0:T(8,128)(2,1)S(1)} fusion(bf16[4,144,6,32]{1,3,2,0:T(8,128)(2,1)S(1)} %bitcast.156, f32[4,6,72]{2,1,0:T(8,128)} %fusion.358, f32[6,72,144]{2,1,0:T(8,128)S(1)} %bitcast.145, bf16[4,144,6,32]{1,3,2,0:T(8,128)(2,1)S(1)} %bitcast.153, bf16[4,72,6,32]{3,2,0,1:T(8,128)(2,1)S(1)} %reshape_reshape.10), kind=kOutput, calls=%fused_computation.47 | convolution fusion | flops 33151824 | bytes 919296 | tf_op jit(solution)/shard_map/whqk,wkhd->wqhd/dot_general | solution.py:107
  114.5 2.4 %fusion.16 = bf16[288,192]{1,0:T(8,128)(2,1)S(1)} fusion(f32[768]{0:T(1024)S(1)} %copy-done.12, bf16[288,192]{1,0:T(8,128)(2,1)S(1)} %fusion.189, bf16[1,768,192]{2,1,0:T(8,128)(2,1)S(1)} %copy-done.1, bf16[1,192,768]{2,1,0:T(8,128)(2,1)S(1)} %copy.78, f32[192]{0:T(256)S(1)} %copy-done.23, f32[288]{0:T(512)S(1)} %add_rsqrt_fusion.4, ...), kind=kOutput, calls=%fused_computation.44 | convolution fusion | flops 185020416 | bytes 818688 | tf_op jit(solution)/shard_map/dot_general | solution.py:127
  116.9 4.7 %collective-permute-start.3 = (bf16[2,3,48,192]{3,2,1,0:T(8,128)(2,1)S(1)}, bf16[2,3,48,192]{3,2,1,0:T(8,128)(2,1)S(1)}, u32[]{:S(2)}, u32[]{:S(2)}) collective-permute-start(bf16[2,3,48,192]{3,2,1,0:T(8,128)(2,1)S(1)} %bitcast.159), channel_id=1, source_target_pairs={{0,16},{1,17},{2,18},{3,19},{4,20},{5,21},{6,22},{7,23},{8,24},{9,... | collective-permute-start | bytes 331784 | tf_op jit(solution)/shard_map/ppermute | solution.py:28
  121.6 2.4 %collective-permute-done.3 = bf16[2,3,48,192]{3,2,1,0:T(8,128)(2,1)S(1)} collective-permute-done((bf16[2,3,48,192]{3,2,1,0:T(8,128)(2,1)S(1)}, bf16[2,3,48,192]{3,2,1,0:T(8,128)(2,1)S(1)}, u32[]{:S(2)}, u32[]{:S(2)}) %collective-permute-start.3) | collective-permute-done | bytes 110624 | tf_op jit(solution)/shard_map/ppermute | solution.py:28
  125.9 5.0 %collective-permute-done.4 = bf16[288,384]{1,0:T(8,128)(2,1)S(1)} collective-permute-done((bf16[288,384]{1,0:T(8,128)(2,1)S(1)}, bf16[288,384]{1,0:T(8,128)(2,1)S(1)}, u32[]{:S(2)}, u32[]{:S(2)}) %collective-permute-start.4) | collective-permute-done | bytes 221216 | tf_op jit(solution)/shard_map/ppermute | solution.py:22
  132.2 1.1 fusion.361
  133.3 3.1 %fusion.20 = bf16[4,72,6,32]{1,3,2,0:T(8,128)(2,1)S(1)} fusion(bf16[4,144,6,32]{1,3,2,0:T(8,128)(2,1)S(1)} %bitcast.154, f32[4,6,72]{2,1,0:T(8,128)S(1)} %fusion.361, f32[6,72,144]{2,1,0:T(8,128)S(1)} %bitcast.147, bf16[4,144,6,32]{1,3,2,0:T(8,128)(2,1)S(1)} %bitcast.149, bf16[4,72,6,32]{3,2,0,1:T(8,128)(2,1)S(1)} %reshape_reshape.11), kind=kOutput, calls=%fused_computation.48 | convolution fusion | flops 33151824 | bytes 919296 | tf_op jit(solution)/shard_map/whqk,wkhd->wqhd/dot_general | solution.py:107
  136.5 0.9 copy.91
  138.4 2.4 %fusion.15 = bf16[288,192]{1,0:T(8,128)(2,1)S(1)} fusion(f32[768]{0:T(1024)S(1)} %copy-done.13, bf16[288,192]{1,0:T(8,128)(2,1)S(1)} %fusion.190, bf16[1,768,192]{2,1,0:T(8,128)(2,1)S(1)} %copy-done.1, bf16[1,192,768]{2,1,0:T(8,128)(2,1)S(1)} %copy.78, f32[192]{0:T(256)S(1)} %copy-done.24, f32[288]{0:T(512)S(1)} %add_rsqrt_fusion.3, ...), kind=kOutput, calls=%fused_computation.43 | convolution fusion | flops 185020416 | bytes 818688 | tf_op jit(solution)/shard_map/dot_general | solution.py:127
  (149 shorter events, 19.1 us)
Async XLA Ops:
  25.9 2.6 %copy-start.9 = (f32[1,1,1,6,1656]{4,2,3,1,0:T(1,128)S(1)}, f32[1,1,1,6,1656]{4,2,3,1,0:T(1,128)}, u32[]{:S(2)}) copy-start(f32[1,1,1,6,1656]{4,2,3,1,0:T(1,128)} %param.28) | copy-start | bytes 119236
  26.2 2.6 %copy-start.8 = (s32[10368]{0:T(1024)S(1)}, s32[10368]{0:T(1024)}, u32[]{:S(2)}) copy-start(s32[10368]{0:T(1024)} %constant.151) | copy-start | bytes 124420
  26.4 51.2 %collective-permute-start = (bf16[288,384]{1,0:T(8,128)(2,1)S(1)}, bf16[288,384]{1,0:T(8,128)(2,1)}, u32[]{:S(2)}, u32[]{:S(2)}) collective-permute-start(bf16[288,384]{1,0:T(8,128)(2,1)S(1)} %slice.62), channel_id=1, source_target_pairs={{0,4},{4,0},{8,12},{12,8},{1,5},{5,1},{9,13},{13,9},{2,6},{6,2},{1... | collective-permute-start | bytes 663560 | tf_op jit(solution)/shard_map/ppermute | solution.py:22
  48.8 4.9 %copy-start.10 = (bf16[1,192,48]{1,2,0:T(8,128)(2,1)S(1)}, bf16[1,192,48]{1,2,0:T(8,128)(2,1)}, u32[]{:S(2)}) copy-start(bf16[1,192,48]{1,2,0:T(8,128)(2,1)} %param.20) | copy-start | bytes 55300
  48.8 11.5 %copy-start.7 = (bf16[1,192,192]{2,1,0:T(8,128)(2,1)S(1)}, bf16[1,192,192]{2,1,0:T(8,128)(2,1)}, u32[]{:S(2)}) copy-start(bf16[1,192,192]{2,1,0:T(8,128)(2,1)} %param.24) | copy-start | bytes 221188
  53.7 23.9 %copy-start.14 = (bf16[1,192]{1,0:T(2,128)(2,1)S(1)}, bf16[1,192]{1,0:T(2,128)(2,1)}, u32[]{:S(2)}) copy-start(bf16[1,192]{1,0:T(2,128)(2,1)} %param.22) | copy-start | bytes 1156
  53.7 23.8 %copy-start.15 = (bf16[1,192]{1,0:T(2,128)(2,1)S(1)}, bf16[1,192]{1,0:T(2,128)(2,1)}, u32[]{:S(2)}) copy-start(bf16[1,192]{1,0:T(2,128)(2,1)} %param.23) | copy-start | bytes 1156
  53.7 23.9 %copy-start = (bf16[2,2,3,48,192]{4,3,2,1,0:T(8,128)(2,1)S(1)}, bf16[2,2,3,48,192]{4,3,2,1,0:T(8,128)(2,1)}, u32[]{:S(2)}) copy-start(bf16[2,2,3,48,192]{4,3,2,1,0:T(8,128)(2,1)} %param.15) | copy-start | bytes 663556
  77.5 10.0 %copy-start.16 = (f32[1,192]{1,0:T(1,128)}, f32[1,192]{1,0:T(1,128)S(1)}, u32[]{:S(2)}) copy-start(f32[1,192]{1,0:T(1,128)S(1)} %mul.170) | copy-start | bytes 2308
  77.5 10.0 %copy-start.19 = (f32[1,192]{1,0:T(1,128)}, f32[1,192]{1,0:T(1,128)S(1)}, u32[]{:S(2)}) copy-start(f32[1,192]{1,0:T(1,128)S(1)} %add.304) | copy-start | bytes 2308
  84.7 2.9 %copy-start.1 = (bf16[1,768,192]{2,1,0:T(8,128)(2,1)S(1)}, bf16[1,768,192]{2,1,0:T(8,128)(2,1)}, u32[]{:S(2)}) copy-start(bf16[1,768,192]{2,1,0:T(8,128)(2,1)} %all_gather.30) | copy-start | bytes 884740
  84.7 2.9 %copy-start.11 = (f32[768]{0:T(1024)S(1)}, f32[768]{0:T(1024)}, u32[]{:S(2)}) copy-start(f32[768]{0:T(1024)} %add.317) | copy-start | bytes 9220
  84.7 2.9 %copy-start.22 = (f32[192]{0:T(256)S(1)}, f32[192]{0:T(256)}, u32[]{:S(2)}) copy-start(f32[192]{0:T(256)} %add.318) | copy-start | bytes 2308
  90.0 7.5 %copy-start.3 = (bf16[288,192]{1,0:T(8,128)(2,1)}, bf16[288,192]{1,0:T(8,128)(2,1)S(1)}, u32[]{:S(2)}) copy-start(bf16[288,192]{1,0:T(8,128)(2,1)S(1)} %fusion.17) | copy-start | bytes 331780
  90.0 7.0 %collective-permute-start.1 = (bf16[2,3,48,192]{3,2,1,0:T(8,128)(2,1)S(1)}, bf16[2,3,48,192]{3,2,1,0:T(8,128)(2,1)S(1)}, u32[]{:S(2)}, u32[]{:S(2)}) collective-permute-start(bf16[2,3,48,192]{3,2,1,0:T(8,128)(2,1)S(1)} %bitcast.157), channel_id=1, source_target_pairs={{0,16},{1,17},{2,18},{3,19},{4,20},{5,21},{6,22},{7,23},{8,24},{9,... | collective-permute-start | bytes 331784 | tf_op jit(solution)/shard_map/ppermute | solution.py:28
  98.0 6.9 %collective-permute-start.2 = (bf16[288,384]{1,0:T(8,128)(2,1)S(1)}, bf16[288,384]{1,0:T(8,128)(2,1)S(1)}, u32[]{:S(2)}, u32[]{:S(2)}) collective-permute-start(bf16[288,384]{1,0:T(8,128)(2,1)S(1)} %slice.66), channel_id=1, source_target_pairs={{0,4},{4,0},{8,12},{12,8},{1,5},{5,1},{9,13},{13,9},{2,6},{6,2},{1... | collective-permute-start | bytes 663560 | tf_op jit(solution)/shard_map/ppermute | solution.py:22
  106.9 1.7 %copy-start.2 = (bf16[4,144,192]{1,2,0:T(8,128)(2,1)S(1)}, bf16[4,144,192]{1,2,0:T(8,128)(2,1)}, u32[]{:S(2)}) copy-start(bf16[4,144,192]{1,2,0:T(8,128)(2,1)} %copy.80) | copy-start | bytes 663556
  112.5 2.0 %copy-start.12 = (f32[768]{0:T(1024)S(1)}, f32[768]{0:T(1024)}, u32[]{:S(2)}) copy-start(f32[768]{0:T(1024)} %add.317) | copy-start | bytes 9220
  112.5 2.0 %copy-start.17 = (f32[1,192]{1,0:T(1,128)S(1)}, f32[1,192]{1,0:T(1,128)}, u32[]{:S(2)}) copy-start(f32[1,192]{1,0:T(1,128)} %copy-done.16) | copy-start | bytes 2308
  112.5 2.0 %copy-start.20 = (f32[1,192]{1,0:T(1,128)S(1)}, f32[1,192]{1,0:T(1,128)}, u32[]{:S(2)}) copy-start(f32[1,192]{1,0:T(1,128)} %copy-done.19) | copy-start | bytes 2308
  112.5 2.0 %copy-start.23 = (f32[192]{0:T(256)S(1)}, f32[192]{0:T(256)}, u32[]{:S(2)}) copy-start(f32[192]{0:T(256)} %add.318) | copy-start | bytes 2308
  116.9 4.7 %copy-start.5 = (bf16[288,192]{1,0:T(8,128)(2,1)}, bf16[288,192]{1,0:T(8,128)(2,1)S(1)}, u32[]{:S(2)}) copy-start(bf16[288,192]{1,0:T(8,128)(2,1)S(1)} %fusion.16) | copy-start | bytes 331780
  116.9 7.1 %collective-permute-start.3 = (bf16[2,3,48,192]{3,2,1,0:T(8,128)(2,1)S(1)}, bf16[2,3,48,192]{3,2,1,0:T(8,128)(2,1)S(1)}, u32[]{:S(2)}, u32[]{:S(2)}) collective-permute-start(bf16[2,3,48,192]{3,2,1,0:T(8,128)(2,1)S(1)} %bitcast.159), channel_id=1, source_target_pairs={{0,16},{1,17},{2,18},{3,19},{4,20},{5,21},{6,22},{7,23},{8,24},{9,... | collective-permute-start | bytes 331784 | tf_op jit(solution)/shard_map/ppermute | solution.py:28
  124.9 6.0 %collective-permute-start.4 = (bf16[288,384]{1,0:T(8,128)(2,1)S(1)}, bf16[288,384]{1,0:T(8,128)(2,1)S(1)}, u32[]{:S(2)}, u32[]{:S(2)}) collective-permute-start(bf16[288,384]{1,0:T(8,128)(2,1)S(1)} %slice.70), channel_id=1, source_target_pairs={{0,4},{4,0},{8,12},{12,8},{1,5},{5,1},{9,13},{13,9},{2,6},{6,2},{1... | collective-permute-start | bytes 663560 | tf_op jit(solution)/shard_map/ppermute | solution.py:22
  136.4 2.0 %copy-start.13 = (f32[768]{0:T(1024)S(1)}, f32[768]{0:T(1024)}, u32[]{:S(2)}) copy-start(f32[768]{0:T(1024)} %add.317) | copy-start | bytes 9220
  136.4 2.0 %copy-start.18 = (f32[1,192]{1,0:T(1,128)S(1)}, f32[1,192]{1,0:T(1,128)}, u32[]{:S(2)}) copy-start(f32[1,192]{1,0:T(1,128)} %copy-done.16) | copy-start | bytes 2308
  136.4 2.0 %copy-start.21 = (f32[1,192]{1,0:T(1,128)S(1)}, f32[1,192]{1,0:T(1,128)}, u32[]{:S(2)}) copy-start(f32[1,192]{1,0:T(1,128)} %copy-done.19) | copy-start | bytes 2308
  136.4 2.0 %copy-start.24 = (f32[192]{0:T(256)S(1)}, f32[192]{0:T(256)}, u32[]{:S(2)}) copy-start(f32[192]{0:T(256)} %add.318) | copy-start | bytes 2308
  138.4 2.4 %copy-start.4 = (bf16[288,192]{1,0:T(8,128)(2,1)S(1)}, bf16[288,192]{1,0:T(8,128)(2,1)}, u32[]{:S(2)}) copy-start(bf16[288,192]{1,0:T(8,128)(2,1)} %copy-done.3) | copy-start | bytes 331780
  138.4 2.4 %copy-start.6 = (bf16[288,192]{1,0:T(8,128)(2,1)S(1)}, bf16[288,192]{1,0:T(8,128)(2,1)}, u32[]{:S(2)}) copy-start(bf16[288,192]{1,0:T(8,128)(2,1)} %copy-done.5) | copy-start | bytes 331780
where the time goes:
time: 142 us
  local copies, waits for them, and re-layouts  40.5 us (29%)
  blocking collectives  36.5 us (26%)
  matrix products  23.6 us (17%)
  waiting for transfers between devices  16.7 us (12%)
  starting transfers between devices  10.9 us (8%)
  other arithmetic  10.6 us (7%)
  between operations  2.86 us (2%)
    gather x2, local copies, waits for them, and re-layouts, on_device(): bias_block = jnp.take(bias_table, table_items, axis=1)  24.8 us
    ppermute x3, waiting for transfers between devices, swapped(): return lax.ppermute(block, axis, route)  11 us
    dot_general x3, matrix products, earth_block(): jnp.einsum('whqk,wkhd->wqhd', probs, value_heads, preferred_element_type=...  10.8 us
    all_gather x1, blocking collectives, on_device(): lax.all_gather(expand_weight, 'tp', axis=2, tiled=True)  8.71 us
    unnamed x1, blocking collectives  8.48 us
    ppermute x2, starting transfers between devices, passed_along(): lax.ppermute(value, axis, [(source, source + steps) for source in range(f...  8.29 us
    all_gather x1, blocking collectives, on_device(): lax.all_gather(reduce_weight, 'tp', axis=1, tiled=True)  7.79 us
    dot_general x3, matrix products, earth_block(): jnp.dot(hidden, reduce_matrix, preferred_element_type=jnp.float32)  7.14 us
  transfers between devices with their start and end apart: 5, of which 4 were waited for; matrix products, arithmetic and copies ran while one was open for 20% of the time, Pallas kernels for 0%

commit v1 on v0

v1 whole, which is shorter than its diff:
```python
import functools

import jax
import jax.numpy as jnp
import numpy as np
from jax import lax
from jax.experimental import pallas as pl
from jax.experimental.pallas import tpu as pltpu
from jax.sharding import PartitionSpec as P

WZ = 2
WH = 6
WW = 12
HALF = WH // 2
GROUP = WZ * HALF
EPS = 1e-05
MESH = pl.DeviceIdType.MESH
F32 = jnp.float32
BF16 = jnp.bfloat16
NT = (((1,), (1,)), ((), ()))


def mm(a, b):
    return jnp.dot(a, b, preferred_element_type=F32)


def mm_nt(a, b):
    return lax.dot_general(a, b, NT, preferred_element_type=F32)


def layer_norm(values, gain, shift):
    mean = jnp.mean(values, axis=-1, keepdims=True)
    centred = values - mean
    spread = jnp.mean(centred * centred, axis=-1, keepdims=True)
    return centred * lax.rsqrt(spread + EPS) * gain + shift


def kernel(
    tp, micro, heads, slabs,
    x_ref, g1_ref, s1_ref, qw_ref, qb_ref, pw_ref, pb_ref, g2_ref, s2_ref,
    ew_ref, eb_ref, rw_ref, rb_ref, table_ref,
    out_ref,
    qkv, proj, expand, reduce, near, inbuf, outp, perm, unperm,
    own_n, near_n, att_n, table, bias,
    w_send, w_recv, f_send, f_recv, o_send, o_recv,
):
    me = lax.axis_index("tp")
    lat = lax.axis_index("lat")
    section = lax.axis_index("section")
    pair = lat + 1 - 2 * lax.rem(lat, 2)
    other = 1 - section
    cells, width = x_ref.shape[1:]
    wide = own_n.shape[1]
    half_cells = cells // slabs
    head_size = width // heads
    q_part, p_part = qw_ref.shape[1], pw_ref.shape[1]
    e_rows = width + 16

    barrier = pltpu.get_barrier_semaphore()
    for k in range(1, tp):
        pl.semaphore_signal(barrier, inc=1, device_id={"tp": lax.rem(me + k, tp)}, device_id_type=MESH)
    pl.semaphore_signal(barrier, inc=1, device_id={"lat": pair}, device_id_type=MESH)
    pl.semaphore_signal(barrier, inc=1, device_id={"section": other}, device_id_type=MESH)
    pl.semaphore_signal(barrier, inc=1, device_id={"section": other, "lat": pair}, device_id_type=MESH)

    tail = lax.broadcasted_iota(jnp.int32, (wide - width, q_part), 0)
    q_own = jnp.concatenate(
        [qw_ref[...].astype(F32), jnp.where(tail == 0, qb_ref[...].astype(F32), 0.0)], axis=0)
    q_rows = pl.ds(pl.multiple_of(me * q_part, 16), q_part)
    qkv[q_rows, :] = q_own.T.astype(BF16)
    tail = lax.broadcasted_iota(jnp.int32, (wide - width, p_part), 0)
    p_own = jnp.concatenate(
        [pw_ref[...].astype(F32),
         jnp.where(tail == 0, pb_ref[...].astype(F32), jnp.where(tail == 1, rb_ref[...].astype(F32), 0.0))],
        axis=0)
    p_rows = pl.ds(pl.multiple_of(me * p_part, 16), p_part)
    proj[p_rows, :] = p_own.T.astype(BF16)
    expand[:, e_rows:, :] = jnp.zeros_like(expand[:, e_rows:, :])
    expand[me, :width, :] = ew_ref[...]
    tail = lax.broadcasted_iota(jnp.int32, (16, width), 0)
    expand[me, width:e_rows, :] = jnp.where(tail == 0, eb_ref[...].astype(F32), 0.0).astype(BF16)
    reduce[me] = rw_ref[...]

    pl.semaphore_wait(barrier, tp + 2)

    def weight_copy(kind, k):
        ref = (
            qkv.at[q_rows, :],
            proj.at[p_rows, :],
            expand.at[me, pl.ds(0, e_rows), :],
            reduce.at[me],
        )[kind]
        return pltpu.make_async_remote_copy(
            src_ref=ref, dst_ref=ref, send_sem=w_send.at[kind, k - 1], recv_sem=w_recv.at[kind, k - 1],
            device_id={"tp": lax.rem(me + k, tp)}, device_id_type=MESH)

    def field_copy():
        return pltpu.make_async_remote_copy(
            src_ref=x_ref, dst_ref=near, send_sem=f_send, recv_sem=f_recv,
            device_id={"lat": pair}, device_id_type=MESH)

    def state_copy(t, which):
        target = {"section": other} if which == 0 else {"section": other, "lat": pair}
        return pltpu.make_async_remote_copy(
            src_ref=outp.at[t], dst_ref=inbuf.at[t, which], send_sem=o_send.at[t, which],
            recv_sem=o_recv.at[t, which], device_id=target, device_id_type=MESH)

    for k in range(1, tp):
        weight_copy(0, k).start()

    @pl.when(section == 0)
    def _():
        field_copy().start()

    for kind in (1, 2, 3):
        for k in range(1, tp):
            weight_copy(kind, k).start()

    stretch = cells // GROUP

    def target_of(j):
        a = sum((j >= stretch * k).astype(jnp.int32) for k in range(1, GROUP))
        return (j - stretch * a) * GROUP + a

    rows = lax.broadcasted_iota(jnp.int32, (cells, cells), 0)
    cols = lax.broadcasted_iota(jnp.int32, (cells, cells), 1)
    perm[...] = (rows == target_of(cols)).astype(F32).astype(BF16)
    unperm[...] = (cols == target_of(rows)).astype(F32).astype(BF16)
    lanes = lax.broadcasted_iota(jnp.int32, (cells, wide), 1)
    ones = (lanes == width).astype(F32).astype(BF16)
    own_n[...] = ones
    near_n[...] = ones
    att_n[...] = ones

    @pl.when(section == 0)
    def _():
        for t in range(micro):
            inbuf[t, 0] = mm(perm[...], x_ref[t]).astype(BF16)

    table[...] = jnp.zeros_like(table)
    span = WH * (2 * WW - 1)
    for zq in range(WZ):
        for zk in range(WZ):
            for r in range(HALF):
                off = ((zq * WZ + zk) * HALF + r) * span
                piece = table_ref[:, off:off + span]
                for h in range(heads):
                    row = h * GROUP + zq * HALF + r
                    table[row:row + 1, zk * 256:zk * 256 + span] = piece[h:h + 1]
    c = lax.broadcasted_iota(jnp.int32, (table.shape[1], 2 * half_cells), 1)
    far = (c >= half_cells).astype(jnp.int32)
    c = c - half_cells * far
    wk = sum((c >= GROUP * k).astype(jnp.int32) for k in range(1, WW))
    zr = c - GROUP * wk
    zk = (zr >= HALF).astype(jnp.int32)
    band = lax.rem(lat, 2)
    hk = zr - HALF * zk + HALF * (band + far - 2 * band * far)
    place = zk * 256 + hk * (2 * WW - 1) + WW - 1 - wk
    pick = (lax.broadcasted_iota(jnp.int32, place.shape, 0) == place).astype(F32).astype(BF16)
    full = table[...]
    lines = full.shape[0]
    for wq in range(WW):
        turned = full if wq == 0 else pltpu.roll(full, full.shape[1] - wq, 1)
        first = turned.astype(BF16)
        rest = turned - first.astype(F32)
        second = rest.astype(BF16)
        third = (rest - second.astype(F32)).astype(BF16)
        parts = mm(jnp.concatenate([first, second, third], axis=0), pick)
        total = parts[:lines] + parts[lines:2 * lines] + parts[2 * lines:]
        for h in range(heads):
            at = h * half_cells + wq * GROUP
            bias[at:at + GROUP, :] = total[h * GROUP:(h + 1) * GROUP]

    @pl.when(section == 0)
    def _():
        field_copy().wait_recv()
        for t in range(micro):
            inbuf[t, 1] = mm(perm[...], near[t]).astype(BF16)

    scale = 1.0 / float(np.sqrt(head_size))
    lane_head = lax.broadcasted_iota(jnp.int32, (half_cells, width), 1)
    in_head = [(lane_head >= h * head_size) & (lane_head < (h + 1) * head_size) for h in range(heads)]

    def weights_here(t, kind):
        @pl.when(t == 0)
        def _():
            for k in range(1, tp):
                weight_copy(kind, k).wait_recv()

    def turn(t, carry):
        @pl.when(section == 1)
        def _():
            state_copy(t, 0).wait_recv()
            state_copy(t, 1).wait_recv()

        g1, s1 = g1_ref[...].astype(F32), s1_ref[...].astype(F32)
        g2, s2 = g2_ref[...].astype(F32), s2_ref[...].astype(F32)
        grid = inbuf[t, 0].astype(F32)
        own_n[:, :width] = layer_norm(grid, g1, s1).astype(BF16)
        near_n[:, :width] = layer_norm(inbuf[t, 1].astype(F32), g1, s1).astype(BF16)
        weights_here(t, 0)
        q = mm_nt(own_n[...], qkv[:width, :])
        k_own = mm_nt(own_n[...], qkv[width:2 * width, :])
        v_own = mm_nt(own_n[...], qkv[2 * width:, :])
        k_near = mm_nt(near_n[...], qkv[width:2 * width, :])
        v_near = mm_nt(near_n[...], qkv[2 * width:, :])
        attended = []
        for s in range(slabs):
            cut = slice(s * half_cells, (s + 1) * half_cells)
            keys = jnp.concatenate([k_own[cut], k_near[cut]], axis=0).astype(BF16)
            vals = jnp.concatenate([v_own[cut], v_near[cut]], axis=0).astype(BF16)
            stack = jnp.concatenate([jnp.where(m, q[cut], 0.0) for m in in_head], axis=0).astype(BF16)
            scores = mm_nt(stack, keys) * scale + bias[...]
            e = jnp.exp(scores - jnp.max(scores, axis=-1, keepdims=True))
            probs = (e * (1.0 / jnp.sum(e, axis=-1, keepdims=True))).astype(BF16)
            mixed = mm(probs, vals)
            total = jnp.zeros((half_cells, width), F32)
            for h, m in enumerate(in_head):
                total = jnp.where(m, mixed[h * half_cells:(h + 1) * half_cells], total)
            attended.append(total)
        att_n[:, :width] = jnp.concatenate(attended, axis=0).astype(BF16)
        weights_here(t, 1)
        middle = (grid + mm_nt(att_n[...], proj[...])).astype(BF16).astype(F32)
        pick_row = (lax.broadcasted_iota(jnp.int32, (16, wide), 1) == width + 1).astype(F32).astype(BF16)
        shift_out = mm_nt(pick_row, proj[...])[:1]
        own_n[:, :width] = layer_norm(middle, g2, s2).astype(BF16)
        weights_here(t, 2)
        result = middle + shift_out
        hidden = []
        for i in range(tp):
            pre = mm(own_n[...], expand[i])
            hidden.append((0.5 * pre * (1.0 + lax.erf(pre * float(np.sqrt(0.5))))).astype(BF16))
        weights_here(t, 3)
        for i in range(tp):
            result = result + mm(hidden[i], reduce[i])
        outp[t] = result.astype(BF16)

        @pl.when(section == 0)
        def _():
            state_copy(t, 0).start()
            state_copy(t, 1).start()

        out_ref[t] = mm(unperm[...], outp[t]).astype(BF16)
        return carry

    lax.fori_loop(0, micro, turn, 0)

    for kind in range(4):
        for k in range(1, tp):
            weight_copy(kind, k).wait_send()

    @pl.when(section == 0)
    def _():
        field_copy().wait_send()
        for t in range(micro):
            state_copy(t, 0).wait_send()
            state_copy(t, 1).wait_send()


def on_device(
    initial_field, first_gain, first_shift, qkv_weight, qkv_bias, proj_weight, proj_bias,
    second_gain, second_shift, expand_weight, expand_bias, reduce_weight, reduce_bias, earth_bias,
):
    tp = lax.axis_size("tp")
    micro, levels, lat_rows, lon, width = initial_field.shape
    cells = levels * lat_rows * lon
    heads, entries = earth_bias.shape[-2:]
    slabs = lon // WW
    half_cells = cells // slabs
    wide = -(-(width + 2) // 128) * 128
    lines = -(-heads * GROUP // 16) * 16
    vmem = pl.BlockSpec(memory_space=pltpu.VMEM)
    dma = pltpu.SemaphoreType.DMA
    out = pl.pallas_call(
        functools.partial(kernel, tp, micro, heads, slabs),
        out_shape=jax.ShapeDtypeStruct((micro, cells, width), BF16),
        in_specs=[vmem] * 14,
        out_specs=vmem,
        scratch_shapes=[
            pltpu.VMEM((3 * width, wide), BF16),
            pltpu.VMEM((width, wide), BF16),
            pltpu.VMEM((tp, wide, width), BF16),
            pltpu.VMEM((tp, width, width), BF16),
            pltpu.VMEM((micro, cells, width), BF16),
            pltpu.VMEM((micro, 2, cells, width), BF16),
            pltpu.VMEM((micro, cells, width), BF16),
            pltpu.VMEM((cells, cells), BF16),
            pltpu.VMEM((cells, cells), BF16),
            pltpu.VMEM((cells, wide), BF16),
            pltpu.VMEM((cells, wide), BF16),
            pltpu.VMEM((cells, wide), BF16),
            pltpu.VMEM((lines, 512), F32),
            pltpu.VMEM((heads * half_cells, 2 * half_cells), F32),
            dma((4, tp - 1)),
            dma((4, tp - 1)),
            dma,
            dma,
            dma((micro, 2)),
            dma((micro, 2)),
        ],
        compiler_params=pltpu.CompilerParams(
            collective_id=0, has_side_effects=True, vmem_limit_bytes=40 * 1024 * 1024),
    )(
        initial_field.reshape(micro, cells, width), first_gain, first_shift, qkv_weight[0], qkv_bias,
        proj_weight[0], proj_bias, second_gain, second_shift, expand_weight[0], expand_bias,
        reduce_weight[0], reduce_bias, earth_bias.reshape(heads, entries),
    )
    return out.reshape(1, micro, levels, lat_rows, lon, width)


def solution(mesh):
    return jax.shard_map(
        on_device,
        mesh=mesh,
        in_specs=(
            P(None, "tp", "lat", None, None),
            P("section", None),
            P("section", None),
            P("section", None, "tp"),
            P("section", "tp"),
            P("section", None, "tp"),
            P("section", "tp"),
            P("section", None),
            P("section", None),
            P("section", None, "tp"),
            P("section", "tp"),
            P("section", "tp", None),
            P("section", "tp"),
            P("section", "tp", "lat", None, None),
        ),
        out_specs=P("section", None, "tp", "lat", None, None),
        check_vma=False,
    )
```

time: 142 us -> 41.2 us (0.29)
  the two profiles are of different devices: /device:TPU:0 before, /device:TPU:19 now
where the time goes in v1:
time: 41.2 us; the launch traced here: 41 us
  Pallas kernels  35.8 us (87%)
  local copies, waits for them, and re-layouts  5.05 us (12%)
    pallas_call x1, Pallas kernels, on_device(): pl.pallas_call(functools.partial(kernel, tp, micro, heads, slabs), out_sh...  35.8 us
    unnamed x28, local copies, waits for them, and re-layouts  5.05 us

profile of v1, /device:TPU:19, one launch (start us, length us, event | category | flops | bytes accessed | tf_op | source)
XLA Modules:
  0.0 41.0 jit_solution(8571384621109515533)
XLA Ops:
  0.0 0.0 copy-start.11
  0.0 0.0 copy-start
  0.0 0.9 %copy.16 = bf16[1,192,48]{2,1,0:T(8,128)(2,1)S(1)} copy(bf16[1,192,48]{1,2,0:T(8,128)(2,1)} %param.19) | data formatting | bytes 36864 | tf_op args[5]
  0.9 0.0 copy-done.11
  0.9 0.0 copy-start.4
  0.9 0.0 copy-start.5
  0.9 0.0 copy-start.6
  1.0 0.0 copy-start.7
  1.0 0.0 copy-start.8
  1.0 0.0 copy-start.10
  1.0 1.0 %copy.15 = bf16[1,192,144]{2,1,0:T(8,128)(2,1)S(1)} copy(bf16[1,192,144]{1,2,0:T(8,128)(2,1)} %param.17) | data formatting | bytes 110592 | tf_op args[3]
  2.0 0.0 copy-start.3
  2.0 0.0 copy-start.9
  2.0 0.0 copy-done
  2.0 0.0 copy-done.4
  2.1 0.0 copy-done.5
  2.1 0.0 copy-done.6
  2.1 0.0 copy-done.7
  2.1 0.0 copy-done.8
  2.1 0.0 copy-done.10
  2.1 0.6 %copy-done.3 = bf16[1,192]{1,0:T(2,128)(2,1)S(1)} copy-done((bf16[1,192]{1,0:T(2,128)(2,1)S(1)}, bf16[1,192]{1,0:T(2,128)(2,1)}, u32[]{:S(2)}) %copy-start.3) | copy-done | bytes 408
  2.7 0.0 copy-done.9
  2.7 0.0 copy-start.1
  2.7 0.9 %copy-done.1 = bf16[1,192,192]{2,1,0:T(8,128)(2,1)S(1)} copy-done((bf16[1,192,192]{2,1,0:T(8,128)(2,1)S(1)}, bf16[1,192,192]{2,1,0:T(8,128)(2,1)}, u32[]{:S(2)}) %copy-start.1) | copy-done | bytes 73752
  3.6 0.0 copy-start.2
  3.6 0.9 %copy-done.2 = bf16[1,192,192]{2,1,0:T(8,128)(2,1)S(1)} copy-done((bf16[1,192,192]{2,1,0:T(8,128)(2,1)S(1)}, bf16[1,192,192]{2,1,0:T(8,128)(2,1)}, u32[]{:S(2)}) %copy-start.2) | copy-done | bytes 73752
  4.5 35.8 %shard_map.136 = bf16[2,288,192]{2,1,0:T(8,128)(2,1)S(1)} custom-call(bf16[2,288,192]{2,1,0:T(8,128)(2,1)S(1)} %bitcast.11, bf16[1,192]{1,0:T(2,128)(2,1)S(1)} %copy-done.3, bf16[1,192]{1,0:T(2,128)(2,1)S(1)} %copy-done.4, bf16[192,144]{1,0:T(8,128)(2,1)S(1)} %bitcast.10, bf16[1,144]{1,0:T(2,128)(2,1)S(1)} %copy-done.5, bf16[192,48]{1,0:T(8,128)(2,1)S(1)} %bitcast.13, ...), custom_call_target="tpu_custom_call" | custom-call | tf_op jit(solution)/shard_map/pallas_call | solution.py:274
  40.2 0.7 %copy.21 = bf16[1,2,2,3,48,192]{5,4,3,2,1,0:T(8,128)(2,1)} copy(bf16[1,2,2,3,48,192]{5,4,3,2,1,0:T(8,128)(2,1)S(1)} %bitcast.9) | data formatting | bytes 442368
  (1 shorter events, 0.0 us)
Async XLA Ops:
  0.0 0.9 %copy-start.11 = (f32[1,1,1,6,1656]{4,2,3,1,0:T(1,128)S(1)}, f32[1,1,1,6,1656]{4,2,3,1,0:T(1,128)}, u32[]{:S(2)}) copy-start(f32[1,1,1,6,1656]{4,2,3,1,0:T(1,128)} %param.27) | copy-start | bytes 119236
  0.0 2.0 %copy-start = (bf16[2,2,3,48,192]{4,3,2,1,0:T(8,128)(2,1)S(1)}, bf16[2,2,3,48,192]{4,3,2,1,0:T(8,128)(2,1)}, u32[]{:S(2)}) copy-start(bf16[2,2,3,48,192]{4,3,2,1,0:T(8,128)(2,1)} %param.14) | copy-start | bytes 663556
  0.9 1.1 %copy-start.4 = (bf16[1,192]{1,0:T(2,128)(2,1)S(1)}, bf16[1,192]{1,0:T(2,128)(2,1)}, u32[]{:S(2)}) copy-start(bf16[1,192]{1,0:T(2,128)(2,1)} %s1_ref.1) | copy-start | bytes 1156
  0.9 1.1 %copy-start.5 = (bf16[1,144]{1,0:T(2,128)(2,1)S(1)}, bf16[1,144]{1,0:T(2,128)(2,1)}, u32[]{:S(2)}) copy-start(bf16[1,144]{1,0:T(2,128)(2,1)} %qb_ref.1) | copy-start | bytes 868
  0.9 1.1 %copy-start.6 = (bf16[1,192]{1,0:T(2,128)(2,1)S(1)}, bf16[1,192]{1,0:T(2,128)(2,1)}, u32[]{:S(2)}) copy-start(bf16[1,192]{1,0:T(2,128)(2,1)} %g2_ref.1) | copy-start | bytes 1156
  1.0 1.1 %copy-start.7 = (bf16[1,192]{1,0:T(2,128)(2,1)S(1)}, bf16[1,192]{1,0:T(2,128)(2,1)}, u32[]{:S(2)}) copy-start(bf16[1,192]{1,0:T(2,128)(2,1)} %s2_ref.1) | copy-start | bytes 1156
  1.0 1.1 %copy-start.8 = (bf16[1,192]{1,0:T(2,128)(2,1)S(1)}, bf16[1,192]{1,0:T(2,128)(2,1)}, u32[]{:S(2)}) copy-start(bf16[1,192]{1,0:T(2,128)(2,1)} %eb_ref.1) | copy-start | bytes 1156
  1.0 1.1 %copy-start.10 = (bf16[1,48]{1,0:T(2,128)(2,1)S(1)}, bf16[1,48]{1,0:T(2,128)(2,1)}, u32[]{:S(2)}) copy-start(bf16[1,48]{1,0:T(2,128)(2,1)} %rb_ref.1) | copy-start | bytes 292
  2.0 0.7 %copy-start.3 = (bf16[1,192]{1,0:T(2,128)(2,1)S(1)}, bf16[1,192]{1,0:T(2,128)(2,1)}, u32[]{:S(2)}) copy-start(bf16[1,192]{1,0:T(2,128)(2,1)} %g1_ref.1) | copy-start | bytes 1156
  2.0 0.7 %copy-start.9 = (bf16[1,48]{1,0:T(2,128)(2,1)S(1)}, bf16[1,48]{1,0:T(2,128)(2,1)}, u32[]{:S(2)}) copy-start(bf16[1,48]{1,0:T(2,128)(2,1)} %pb_ref.1) | copy-start | bytes 292
  2.7 0.9 %copy-start.1 = (bf16[1,192,192]{2,1,0:T(8,128)(2,1)S(1)}, bf16[1,192,192]{2,1,0:T(8,128)(2,1)}, u32[]{:S(2)}) copy-start(bf16[1,192,192]{2,1,0:T(8,128)(2,1)} %param.23) | copy-start | bytes 221188
  3.6 0.9 %copy-start.2 = (bf16[1,192,192]{2,1,0:T(8,128)(2,1)S(1)}, bf16[1,192,192]{2,1,0:T(8,128)(2,1)}, u32[]{:S(2)}) copy-start(bf16[1,192,192]{2,1,0:T(8,128)(2,1)} %param.25) | copy-start | bytes 221188

commit v2 on v1

v2 whole, which is shorter than its diff:
```python
import functools

import jax
import jax.numpy as jnp
import numpy as np
from jax import lax
from jax.experimental import pallas as pl
from jax.experimental.pallas import tpu as pltpu
from jax.sharding import PartitionSpec as P

WZ = 2
WH = 6
WW = 12
HALF = WH // 2
GROUP = WZ * HALF
EPS = 1e-05
MESH = pl.DeviceIdType.MESH
F32 = jnp.float32
BF16 = jnp.bfloat16
NT = (((1,), (1,)), ((), ()))


def mm(a, b):
    return jnp.dot(a, b, preferred_element_type=F32)


def mm_nt(a, b):
    return lax.dot_general(a, b, NT, preferred_element_type=F32)


def layer_norm(values, gain, shift):
    mean = jnp.mean(values, axis=-1, keepdims=True)
    centred = values - mean
    spread = jnp.mean(centred * centred, axis=-1, keepdims=True)
    return centred * lax.rsqrt(spread + EPS) * gain + shift


def kernel(
    tp, micro, heads, slabs,
    x_in, g1_in, s1_in, qw_in, qb_in, pw_in, pb_in, g2_in, s2_in,
    ew_in, eb_in, rw_in, rb_in, table_in,
    out_ref,
    x_ref, g1_ref, s1_ref, qw_ref, qb_ref, pw_ref, pb_ref, g2_ref, s2_ref,
    ew_ref, eb_ref, rb_ref, table_ref,
    qkv, proj, expand, reduce, near, inbuf, outp, perm, unperm,
    own_n, near_n, att_n, table, bias,
    l_sem, w_send, w_recv, f_send, f_recv, o_send, o_recv,
):
    me = lax.axis_index("tp")
    lat = lax.axis_index("lat")
    section = lax.axis_index("section")
    pair = lat + 1 - 2 * lax.rem(lat, 2)
    other = 1 - section
    cells, width = x_ref.shape[1:]
    wide = own_n.shape[1]
    half_cells = cells // slabs
    head_size = width // heads
    q_part, p_part = qw_ref.shape[0], pw_ref.shape[0]
    e_rows = width + 16
    core_peer = me + 1 - 2 * lax.rem(me, 2)
    chip_peer = lax.rem(me + tp // 2, tp)

    barrier = pltpu.get_barrier_semaphore()
    pl.semaphore_signal(barrier, inc=1, device_id={"tp": core_peer}, device_id_type=MESH)
    pl.semaphore_signal(barrier, inc=1, device_id={"tp": chip_peer}, device_id_type=MESH)
    pl.semaphore_signal(barrier, inc=1, device_id={"lat": pair}, device_id_type=MESH)
    pl.semaphore_signal(barrier, inc=1, device_id={"section": other}, device_id_type=MESH)
    pl.semaphore_signal(barrier, inc=1, device_id={"section": other, "lat": pair}, device_id_type=MESH)

    loads = [
        pltpu.make_async_copy(source, target, l_sem.at[n])
        for n, (source, target) in enumerate((
            (qw_in, qw_ref), (qb_in, qb_ref), (pw_in, pw_ref), (pb_in, pb_ref), (rb_in, rb_ref),
            (ew_in, ew_ref), (eb_in, eb_ref), (rw_in, reduce.at[me]), (x_in, x_ref), (table_in, table_ref),
            (g1_in, g1_ref), (s1_in, s1_ref), (g2_in, g2_ref), (s2_in, s2_ref),
        ))
    ]
    for load in loads:
        load.start()

    expand[:, e_rows:, :] = jnp.zeros_like(expand[:, e_rows:, :])

    def owner_rows(owner, part):
        return pl.ds(pl.multiple_of(owner * part, 16), part)

    for load in loads[:5]:
        load.wait()
    tail = lax.broadcasted_iota(jnp.int32, (wide - width, q_part), 0)
    q_tail = jnp.where(tail == 0, qb_ref[...].astype(F32), 0.0).T
    qkv[owner_rows(me, q_part), :] = jnp.concatenate(
        [qw_ref[...].astype(F32), q_tail], axis=1).astype(BF16)
    tail = lax.broadcasted_iota(jnp.int32, (wide - width, p_part), 0)
    p_tail = jnp.where(
        tail == 0, pb_ref[...].astype(F32), jnp.where(tail == 1, rb_ref[...].astype(F32), 0.0)).T
    proj[owner_rows(me, p_part), :] = jnp.concatenate(
        [pw_ref[...].astype(F32), p_tail], axis=1).astype(BF16)
    for load in loads[5:8]:
        load.wait()
    expand[me, :width, :] = ew_ref[...]
    tail = lax.broadcasted_iota(jnp.int32, (16, width), 0)
    expand[me, width:e_rows, :] = jnp.where(tail == 0, eb_ref[...].astype(F32), 0.0).astype(BF16)

    pl.semaphore_wait(barrier, 5)

    def weight_copy(kind, way):
        owner = chip_peer if way == 2 else me
        ref = (
            lambda: qkv.at[owner_rows(owner, q_part), :],
            lambda: proj.at[owner_rows(owner, p_part), :],
            lambda: expand.at[owner, pl.ds(0, e_rows), :],
            lambda: reduce.at[owner],
        )[kind]()
        return pltpu.make_async_remote_copy(
            src_ref=ref, dst_ref=ref, send_sem=w_send.at[kind, way], recv_sem=w_recv.at[kind, way],
            device_id={"tp": chip_peer if way == 1 else core_peer}, device_id_type=MESH)

    def hand_on(kind):
        weight_copy(kind, 1).wait_recv()
        weight_copy(kind, 2).start()

    def field_copy():
        return pltpu.make_async_remote_copy(
            src_ref=x_in, dst_ref=near, send_sem=f_send, recv_sem=f_recv,
            device_id={"lat": pair}, device_id_type=MESH)

    chunks = o_send.shape[2]
    chunk = cells // chunks

    def state_copy(t, which, part):
        rows = pl.ds(part * chunk, chunk)
        target = {"section": other} if which == 0 else {"section": other, "lat": pair}
        return pltpu.make_async_remote_copy(
            src_ref=outp.at[t, rows], dst_ref=inbuf.at[t, which, rows], send_sem=o_send.at[t, which, part],
            recv_sem=o_recv.at[t, which, part], device_id=target, device_id_type=MESH)

    def state_forward(t, part):
        rows = pl.ds(part * chunk, chunk)
        return pltpu.make_async_remote_copy(
            src_ref=inbuf.at[t, 0, rows], dst_ref=inbuf.at[t, 1, rows], send_sem=o_send.at[t, 1, part],
            recv_sem=o_recv.at[t, 1, part], device_id={"lat": pair}, device_id_type=MESH)

    for way in (0, 1):
        weight_copy(0, way).start()

    @pl.when(section == 0)
    def _():
        field_copy().start()

    for kind in (1, 2, 3):
        for way in (0, 1):
            weight_copy(kind, way).start()
    for load in loads[8:]:
        load.wait()

    stretch = cells // GROUP
    step = -(-65536 // GROUP)
    line = lax.broadcasted_iota(jnp.int32, (1, cells), 1)
    level_row = sum((line >= stretch * k).astype(jnp.int32) for k in range(1, GROUP))
    forth = (line - stretch * level_row) * GROUP + level_row
    column = lax.shift_right_logical(line * step, 16)
    back = (line - GROUP * column) * stretch + column
    rows = lax.broadcasted_iota(jnp.int32, (cells, cells), 0)
    perm[...] = (rows == forth).astype(F32).astype(BF16)
    unperm[...] = (rows == back).astype(F32).astype(BF16)
    lanes = lax.broadcasted_iota(jnp.int32, (cells, wide), 1)
    ones = (lanes == width).astype(F32).astype(BF16)
    own_n[...] = ones
    near_n[...] = ones
    att_n[...] = ones

    @pl.when(section == 0)
    def _():
        for t in range(micro):
            inbuf[t, 0] = mm(perm[...], x_ref[t]).astype(BF16)

    table[...] = jnp.zeros_like(table)
    span = WH * (2 * WW - 1)
    for zq in range(WZ):
        for zk in range(WZ):
            for r in range(HALF):
                off = ((zq * WZ + zk) * HALF + r) * span
                piece = table_ref[:, 0, off:off + span]
                for h in range(heads):
                    row = h * GROUP + zq * HALF + r
                    table[row:row + 1, zk * span:(zk + 1) * span] = piece[h:h + 1]
    c = lax.broadcasted_iota(jnp.int32, (1, 2 * half_cells), 1)
    far = (c >= half_cells).astype(jnp.int32)
    c = c - half_cells * far
    wk = sum((c >= GROUP * k).astype(jnp.int32) for k in range(1, WW))
    zr = c - GROUP * wk
    zk = (zr >= HALF).astype(jnp.int32)
    band = lax.rem(lat, 2)
    hk = zr - HALF * zk + HALF * (band + far - 2 * band * far)
    place = zk * span + hk * (2 * WW - 1) + WW - 1 - wk
    pick = (lax.broadcasted_iota(jnp.int32, (table.shape[1], 2 * half_cells), 0) == place).astype(F32).astype(BF16)
    full = table[...]
    lines = full.shape[0]
    for wq in range(WW):
        turned = full if wq == 0 else pltpu.roll(full, full.shape[1] - wq, 1)
        first = turned.astype(BF16)
        rest = turned - first.astype(F32)
        second = rest.astype(BF16)
        third = (rest - second.astype(F32)).astype(BF16)
        parts = mm(
            jnp.concatenate([p.astype(F32) for p in (first, second, third)], axis=0).astype(BF16), pick)
        total = parts[:lines] + parts[lines:2 * lines] + parts[2 * lines:]
        for h in range(heads):
            at = h * half_cells + wq * GROUP
            bias[at:at + GROUP, :] = total[h * GROUP:(h + 1) * GROUP]

    hand_on(0)
    hand_on(1)

    @pl.when(section == 0)
    def _():
        field_copy().wait_recv()
        for t in range(micro):
            inbuf[t, 1] = mm(perm[...], near[t]).astype(BF16)

    scale = 1.0 / float(np.sqrt(head_size))
    lane_head = lax.broadcasted_iota(jnp.int32, (half_cells, width), 1)
    in_head = [(lane_head >= h * head_size) & (lane_head < (h + 1) * head_size) for h in range(heads)]

    def weights_here(t, kind):
        @pl.when(t == 0)
        def _():
            weight_copy(kind, 0).wait_recv()
            weight_copy(kind, 2).wait_recv()

    def turn(t, carry):
        @pl.when(section == 1)
        def _():
            for part in range(chunks):
                state_copy(t, 0, part).wait_recv()
                if part < chunks - 1:
                    state_forward(t, part).start()
            for part in range(chunks):
                state_copy(t, 1, part).wait_recv()

        g1, s1 = g1_ref[...].astype(F32), s1_ref[...].astype(F32)
        g2, s2 = g2_ref[...].astype(F32), s2_ref[...].astype(F32)
        grid = inbuf[t, 0].astype(F32)
        own_n[:, :width] = layer_norm(grid, g1, s1).astype(BF16)
        near_n[:, :width] = layer_norm(inbuf[t, 1].astype(F32), g1, s1).astype(BF16)
        weights_here(t, 0)
        q = mm_nt(own_n[...], qkv[:width, :])
        k_own = mm_nt(own_n[...], qkv[width:2 * width, :])
        v_own = mm_nt(own_n[...], qkv[2 * width:, :])
        k_near = mm_nt(near_n[...], qkv[width:2 * width, :])
        v_near = mm_nt(near_n[...], qkv[2 * width:, :])
        attended = []
        for s in range(slabs):
            cut = slice(s * half_cells, (s + 1) * half_cells)
            keys = jnp.concatenate([k_own[cut], k_near[cut]], axis=0).astype(BF16)
            vals = jnp.concatenate([v_own[cut], v_near[cut]], axis=0).astype(BF16)
            stack = jnp.concatenate([jnp.where(m, q[cut], 0.0) for m in in_head], axis=0).astype(BF16)
            scores = mm_nt(stack, keys) * scale + bias[...]
            e = jnp.exp(scores - jnp.max(scores, axis=-1, keepdims=True))
            probs = (e * (1.0 / jnp.sum(e, axis=-1, keepdims=True))).astype(BF16)
            mixed = mm(probs, vals)
            total = jnp.zeros((half_cells, width), F32)
            for h, m in enumerate(in_head):
                total = jnp.where(m, mixed[h * half_cells:(h + 1) * half_cells], total)
            attended.append(total)
            if s % 2 == 1:
                @pl.when(t == 0)
                def _():
                    hand_on(2 + s // 2)
        att_n[:, :width] = jnp.concatenate(attended, axis=0).astype(BF16)
        weights_here(t, 1)
        middle = (grid + mm_nt(att_n[...], proj[...])).astype(BF16).astype(F32)
        pick_row = (lax.broadcasted_iota(jnp.int32, (16, wide), 1) == width + 1).astype(F32).astype(BF16)
        shift_out = mm_nt(pick_row, proj[...])[:1]
        own_n[:, :width] = layer_norm(middle, g2, s2).astype(BF16)
        weights_here(t, 2)
        weights_here(t, 3)
        for part in range(chunks):
            cut = slice(part * chunk, (part + 1) * chunk)
            result = middle[cut] + shift_out
            for i in range(tp):
                pre = mm(own_n[cut, :], expand[i])
                hidden = (0.5 * pre * (1.0 + lax.erf(pre * float(np.sqrt(0.5))))).astype(BF16)
                result = result + mm(hidden, reduce[i])
            outp[t, cut, :] = result.astype(BF16)

            @pl.when(section == 0)
            def _():
                state_copy(t, 0, part).start()
                if part == chunks - 1:
                    state_copy(t, 1, part).start()

        out_ref[t] = mm(unperm[...], outp[t]).astype(BF16)
        return carry

    lax.fori_loop(0, micro, turn, 0)

    for kind in range(4):
        for way in range(3):
            weight_copy(kind, way).wait_send()

    @pl.when(section == 0)
    def _():
        field_copy().wait_send()
        for t in range(micro):
            for part in range(chunks):
                state_copy(t, 0, part).wait_send()
            state_copy(t, 1, chunks - 1).wait_send()

    @pl.when(section == 1)
    def _():
        for t in range(micro):
            for part in range(chunks - 1):
                state_forward(t, part).wait_send()


def on_device(
    initial_field, first_gain, first_shift, qkv_weight, qkv_bias, proj_weight, proj_bias,
    second_gain, second_shift, expand_weight, expand_bias, reduce_weight, reduce_bias, earth_bias,
):
    tp = lax.axis_size("tp")
    micro, levels, lat_rows, lon, width = initial_field.shape
    cells = levels * lat_rows * lon
    heads, entries = earth_bias.shape[-2:]
    slabs = lon // WW
    half_cells = cells // slabs
    wide = -(-(width + 2) // 128) * 128
    lines = -(-heads * GROUP // 8) * 8
    chunks = 2
    lanes = -(-WZ * WH * (2 * WW - 1) // 128) * 128
    q_weight, p_weight = qkv_weight[0].T, proj_weight[0].T
    vmem = pl.BlockSpec(memory_space=pltpu.VMEM)
    dma = pltpu.SemaphoreType.DMA
    out = pl.pallas_call(
        functools.partial(kernel, tp, micro, heads, slabs),
        out_shape=jax.ShapeDtypeStruct((micro, cells, width), BF16),
        in_specs=[pl.BlockSpec(memory_space=pltpu.HBM)] * 14,
        out_specs=vmem,
        scratch_shapes=[
            pltpu.VMEM((micro, cells, width), BF16),
            pltpu.VMEM((1, width), BF16),
            pltpu.VMEM((1, width), BF16),
            pltpu.VMEM(q_weight.shape, BF16),
            pltpu.VMEM(qkv_bias.shape, BF16),
            pltpu.VMEM(p_weight.shape, BF16),
            pltpu.VMEM(proj_bias.shape, BF16),
            pltpu.VMEM((1, width), BF16),
            pltpu.VMEM((1, width), BF16),
            pltpu.VMEM((width, width), BF16),
            pltpu.VMEM((1, width), BF16),
            pltpu.VMEM(reduce_bias.shape, BF16),
            pltpu.VMEM((heads, 1, entries), F32),
            pltpu.VMEM((3 * width, wide), BF16),
            pltpu.VMEM((width, wide), BF16),
            pltpu.VMEM((tp, wide, width), BF16),
            pltpu.VMEM((tp, width, width), BF16),
            pltpu.VMEM((micro, cells, width), BF16),
            pltpu.VMEM((micro, 2, cells, width), BF16),
            pltpu.VMEM((micro, cells, width), BF16),
            pltpu.VMEM((cells, cells), BF16),
            pltpu.VMEM((cells, cells), BF16),
            pltpu.VMEM((cells, wide), BF16),
            pltpu.VMEM((cells, wide), BF16),
            pltpu.VMEM((cells, wide), BF16),
            pltpu.VMEM((lines, lanes), F32),
            pltpu.VMEM((heads * half_cells, 2 * half_cells), F32),
            dma((14,)),
            dma((4, 3)),
            dma((4, 3)),
            dma,
            dma,
            dma((micro, 2, chunks)),
            dma((micro, 2, chunks)),
        ],
        compiler_params=pltpu.CompilerParams(
            collective_id=0, has_side_effects=True, vmem_limit_bytes=60 * 1024 * 1024),
    )(
        initial_field.reshape(micro, cells, width), first_gain, first_shift, q_weight, qkv_bias,
        p_weight, proj_bias, second_gain, second_shift, expand_weight[0], expand_bias,
        reduce_weight[0], reduce_bias, earth_bias.reshape(heads, 1, entries),
    )
    return out.reshape(1, micro, levels, lat_rows, lon, width)


def solution(mesh):
    return jax.shard_map(
        on_device,
        mesh=mesh,
        in_specs=(
            P(None, "tp", "lat", None, None),
            P("section", None),
            P("section", None),
            P("section", None, "tp"),
            P("section", "tp"),
            P("section", None, "tp"),
            P("section", "tp"),
            P("section", None),
            P("section", None),
            P("section", None, "tp"),
            P("section", "tp"),
            P("section", "tp", None),
            P("section", "tp"),
            P("section", "tp", "lat", None, None),
        ),
        out_specs=P("section", None, "tp", "lat", None, None),
        check_vma=False,
    )
```

time: 41.2 us -> 37.5 us (0.910)
  the two profiles are of different devices: /device:TPU:19 before, /device:TPU:11 now
where the time goes in v2:
time: 37.5 us; the launch traced here: 37.3 us
  Pallas kernels  35.6 us (95%)
  local copies, waits for them, and re-layouts  1.69 us (5%)
    pallas_call x1, Pallas kernels, on_device(): pl.pallas_call(functools.partial(kernel, tp, micro, heads, slabs), out_sh...  35.6 us
    unnamed x1, local copies, waits for them, and re-layouts  1.69 us

profile of v2, /device:TPU:11, one launch (start us, length us, event | category | flops | bytes accessed | tf_op | source)
XLA Modules:
  0.0 37.3 jit_solution(6676216726801829097)
XLA Ops:
  0.0 35.6 %shard_map.136 = bf16[2,288,192]{2,1,0:T(8,128)(2,1)} custom-call(bf16[2,288,192]{2,1,0:T(8,128)(2,1)} %bitcast.12, bf16[1,192]{1,0:T(2,128)(2,1)} %g1_in.1, bf16[1,192]{1,0:T(2,128)(2,1)} %s1_in.1, bf16[144,192]{1,0:T(8,128)(2,1)} %bitcast.15, bf16[1,144]{1,0:T(2,128)(2,1)} %qb_in.1, bf16[48,192]{1,0:T(8,128)(2,1)} %bitcast.17, bf16[1,48]{1,0:T(2,128)(2,1)} %pb_in.1, ...), custom_call_target="tpu_custom_call" | custom-call | tf_op jit(solution)/shard_map/pallas_call | solution.py:333
  35.6 1.7 %copy.16 = bf16[1,2,2,3,48,192]{5,4,3,2,1,0:T(8,128)(2,1)} copy(bf16[1,2,2,3,48,192]{5,4,3,2,1,0:T(8,128)(2,1)} %bitcast.11) | data formatting | bytes 442368

commit v3 on v2

--- a/solution.py
+++ b/solution.py
@@ -18,6 +18,8 @@
 F32 = jnp.float32
 BF16 = jnp.bfloat16
 NT = (((1,), (1,)), ((), ()))
+TN = (((0,), (0,)), ((), ()))
+LOG2E = float(np.log2(np.e))
 
 
 def mm(a, b):
@@ -36,14 +38,14 @@
 
 
 def kernel(
-    tp, micro, heads, slabs,
+    tp, micro, heads, slabs, edges,
     x_in, g1_in, s1_in, qw_in, qb_in, pw_in, pb_in, g2_in, s2_in,
     ew_in, eb_in, rw_in, rb_in, table_in,
     out_ref,
     x_ref, g1_ref, s1_ref, qw_ref, qb_ref, pw_ref, pb_ref, g2_ref, s2_ref,
     ew_ref, eb_ref, rb_ref, table_ref,
     qkv, proj, expand, reduce, near, inbuf, outp, perm, unperm,
-    own_n, near_n, att_n, table, bias,
+    own_n, near_n, att_n, table, spread, bias,
     l_sem, w_send, w_recv, f_send, f_recv, o_send, o_recv,
 ):
     me = lax.axis_index("tp")
@@ -55,8 +57,7 @@
     wide = own_n.shape[1]
     half_cells = cells // slabs
     head_size = width // heads
-    q_part, p_part = qw_ref.shape[0], pw_ref.shape[0]
-    e_rows = width + 16
+    q_part, p_part, e_part = qw_ref.shape[0], pw_ref.shape[0], ew_ref.shape[1]
     core_peer = me + 1 - 2 * lax.rem(me, 2)
     chip_peer = lax.rem(me + tp // 2, tp)
 
@@ -71,14 +72,13 @@
         pltpu.make_async_copy(source, target, l_sem.at[n])
         for n, (source, target) in enumerate((
             (qw_in, qw_ref), (qb_in, qb_ref), (pw_in, pw_ref), (pb_in, pb_ref), (rb_in, rb_ref),
-            (ew_in, ew_ref), (eb_in, eb_ref), (rw_in, reduce.at[me]), (x_in, x_ref), (table_in, table_ref),
+            (ew_in, ew_ref), (eb_in, eb_ref), (rw_in, reduce.at[pl.ds(pl.multiple_of(me * e_part, 16), e_part), :]), (x_in, x_ref), (table_in, table_ref),
             (g1_in, g1_ref), (s1_in, s1_ref), (g2_in, g2_ref), (s2_in, s2_ref),
         ))
     ]
     for load in loads:
         load.start()
 
-    expand[:, e_rows:, :] = jnp.zeros_like(expand[:, e_rows:, :])
 
     def owner_rows(owner, part):
         return pl.ds(pl.multiple_of(owner * part, 16), part)
@@ -96,9 +96,9 @@
         [pw_ref[...].astype(F32), p_tail], axis=1).astype(BF16)
     for load in loads[5:8]:
         load.wait()
-    expand[me, :width, :] = ew_ref[...]
-    tail = lax.broadcasted_iota(jnp.int32, (16, width), 0)
-    expand[me, width:e_rows, :] = jnp.where(tail == 0, eb_ref[...].astype(F32), 0.0).astype(BF16)
+    tail = lax.broadcasted_iota(jnp.int32, (wide - width, e_part), 0)
+    expand[owner_rows(me, e_part), :] = jnp.concatenate(
+        [ew_ref[...].astype(F32), jnp.where(tail == 0, eb_ref[...].astype(F32), 0.0)], axis=0).T.astype(BF16)
 
     pl.semaphore_wait(barrier, 5)
 
@@ -107,8 +107,8 @@
         ref = (
             lambda: qkv.at[owner_rows(owner, q_part), :],
             lambda: proj.at[owner_rows(owner, p_part), :],
-            lambda: expand.at[owner, pl.ds(0, e_rows), :],
-            lambda: reduce.at[owner],
+            lambda: expand.at[owner_rows(owner, e_part), :],
+            lambda: reduce.at[owner_rows(owner, e_part), :],
         )[kind]()
         return pltpu.make_async_remote_copy(
             src_ref=ref, dst_ref=ref, send_sem=w_send.at[kind, way], recv_sem=w_recv.at[kind, way],
@@ -123,18 +123,17 @@
             src_ref=x_in, dst_ref=near, send_sem=f_send, recv_sem=f_recv,
             device_id={"lat": pair}, device_id_type=MESH)
 
-    chunks = o_send.shape[2]
-    chunk = cells // chunks
+    chunks = len(edges) - 1
 
     def state_copy(t, which, part):
-        rows = pl.ds(part * chunk, chunk)
+        rows = pl.ds(edges[part], edges[part + 1] - edges[part])
         target = {"section": other} if which == 0 else {"section": other, "lat": pair}
         return pltpu.make_async_remote_copy(
             src_ref=outp.at[t, rows], dst_ref=inbuf.at[t, which, rows], send_sem=o_send.at[t, which, part],
             recv_sem=o_recv.at[t, which, part], device_id=target, device_id_type=MESH)
 
     def state_forward(t, part):
-        rows = pl.ds(part * chunk, chunk)
+        rows = pl.ds(edges[part], edges[part + 1] - edges[part])
         return pltpu.make_async_remote_copy(
             src_ref=inbuf.at[t, 0, rows], dst_ref=inbuf.at[t, 1, rows], send_sem=o_send.at[t, 1, part],
             recv_sem=o_recv.at[t, 1, part], device_id={"lat": pair}, device_id_type=MESH)
@@ -172,6 +171,8 @@
     def _():
         for t in range(micro):
             inbuf[t, 0] = mm(perm[...], x_ref[t]).astype(BF16)
+
+    hand_on(0)
 
     table[...] = jnp.zeros_like(table)
     span = WH * (2 * WW - 1)
@@ -206,9 +207,9 @@
         total = parts[:lines] + parts[lines:2 * lines] + parts[2 * lines:]
         for h in range(heads):
             at = h * half_cells + wq * GROUP
-            bias[at:at + GROUP, :] = total[h * GROUP:(h + 1) * GROUP]
-
-    hand_on(0)
+            spread[at:at + GROUP, :] = total[h * GROUP:(h + 1) * GROUP]
+    bias[...] = spread[...].T * LOG2E
+
     hand_on(1)
 
     @pl.when(section == 0)
@@ -217,7 +218,7 @@
         for t in range(micro):
             inbuf[t, 1] = mm(perm[...], near[t]).astype(BF16)
 
-    scale = 1.0 / float(np.sqrt(head_size))
+    scale = LOG2E / float(np.sqrt(head_size))
     lane_head = lax.broadcasted_iota(jnp.int32, (half_cells, width), 1)
     in_head = [(lane_head >= h * head_size) & (lane_head < (h + 1) * head_size) for h in range(heads)]
 
@@ -234,18 +235,22 @@
                 state_copy(t, 0, part).wait_recv()
                 if part < chunks - 1:
                     state_forward(t, part).start()
-            for part in range(chunks):
-                state_copy(t, 1, part).wait_recv()
 
         g1, s1 = g1_ref[...].astype(F32), s1_ref[...].astype(F32)
         g2, s2 = g2_ref[...].astype(F32), s2_ref[...].astype(F32)
         grid = inbuf[t, 0].astype(F32)
         own_n[:, :width] = layer_norm(grid, g1, s1).astype(BF16)
-        near_n[:, :width] = layer_norm(inbuf[t, 1].astype(F32), g1, s1).astype(BF16)
         weights_here(t, 0)
         q = mm_nt(own_n[...], qkv[:width, :])
         k_own = mm_nt(own_n[...], qkv[width:2 * width, :])
         v_own = mm_nt(own_n[...], qkv[2 * width:, :])
+
+        @pl.when(section == 1)
+        def _():
+            for part in range(chunks):
+                state_copy(t, 1, part).wait_recv()
+
+        near_n[:, :width] = layer_norm(inbuf[t, 1].astype(F32), g1, s1).astype(BF16)
         k_near = mm_nt(near_n[...], qkv[width:2 * width, :])
         v_near = mm_nt(near_n[...], qkv[2 * width:, :])
         attended = []
@@ -254,15 +259,15 @@
             keys = jnp.concatenate([k_own[cut], k_near[cut]], axis=0).astype(BF16)
             vals = jnp.concatenate([v_own[cut], v_near[cut]], axis=0).astype(BF16)
             stack = jnp.concatenate([jnp.where(m, q[cut], 0.0) for m in in_head], axis=0).astype(BF16)
-            scores = mm_nt(stack, keys) * scale + bias[...]
-            e = jnp.exp(scores - jnp.max(scores, axis=-1, keepdims=True))
-            probs = (e * (1.0 / jnp.sum(e, axis=-1, keepdims=True))).astype(BF16)
-            mixed = mm(probs, vals)
+            scores = mm_nt(keys, stack) * scale + bias[...]
+            e = jnp.exp2(scores - jnp.max(scores, axis=0, keepdims=True))
+            probs = (e * (1.0 / jnp.sum(e, axis=0, keepdims=True))).astype(BF16)
+            mixed = lax.dot_general(probs, vals, TN, preferred_element_type=F32)
             total = jnp.zeros((half_cells, width), F32)
             for h, m in enumerate(in_head):
                 total = jnp.where(m, mixed[h * half_cells:(h + 1) * half_cells], total)
             attended.append(total)
-            if s % 2 == 1:
+            if s in (0, 2):
                 @pl.when(t == 0)
                 def _():
                     hand_on(2 + s // 2)
@@ -273,14 +278,13 @@
         shift_out = mm_nt(pick_row, proj[...])[:1]
         own_n[:, :width] = layer_norm(middle, g2, s2).astype(BF16)
         weights_here(t, 2)
-        weights_here(t, 3)
         for part in range(chunks):
-            cut = slice(part * chunk, (part + 1) * chunk)
-            result = middle[cut] + shift_out
-            for i in range(tp):
-                pre = mm(own_n[cut, :], expand[i])
-                hidden = (0.5 * pre * (1.0 + lax.erf(pre * float(np.sqrt(0.5))))).astype(BF16)
-                result = result + mm(hidden, reduce[i])
+            cut = slice(edges[part], edges[part + 1])
+            pre = mm_nt(own_n[cut, :], expand[...])
+            hidden = (0.5 * pre * (1.0 + lax.erf(pre * float(np.sqrt(0.5))))).astype(BF16)
+            if part == 0:
+                weights_here(t, 3)
+            result = middle[cut] + shift_out + mm(hidden, reduce[...])
             outp[t, cut, :] = result.astype(BF16)
 
             @pl.when(section == 0)
@@ -323,15 +327,18 @@
     heads, entries = earth_bias.shape[-2:]
     slabs = lon // WW
     half_cells = cells // slabs
+    hidden = expand_weight.shape[2]
     wide = -(-(width + 2) // 128) * 128
     lines = -(-heads * GROUP // 8) * 8
-    chunks = 2
+    tiles = cells // 16
+    edges = (0, tiles // 2 * 16, (tiles - tiles // 6) * 16, cells)
+    chunks = len(edges) - 1
     lanes = -(-WZ * WH * (2 * WW - 1) // 128) * 128
     q_weight, p_weight = qkv_weight[0].T, proj_weight[0].T
     vmem = pl.BlockSpec(memory_space=pltpu.VMEM)
     dma = pltpu.SemaphoreType.DMA
     out = pl.pallas_call(
-        functools.partial(kernel, tp, micro, heads, slabs),
+        functools.partial(kernel, tp, micro, heads, slabs, edges),
         out_shape=jax.ShapeDtypeStruct((micro, cells, width), BF16),
         in_specs=[pl.BlockSpec(memory_space=pltpu.HBM)] * 14,
         out_specs=vmem,
@@ -345,14 +352,14 @@
             pltpu.VMEM(proj_bias.shape, BF16),
             pltpu.VMEM((1, width), BF16),
             pltpu.VMEM((1, width), BF16),
-            pltpu.VMEM((width, width), BF16),
-            pltpu.VMEM((1, width), BF16),
+            pltpu.VMEM((width, hidden), BF16),
+            pltpu.VMEM((1, hidden), BF16),
             pltpu.VMEM(reduce_bias.shape, BF16),
             pltpu.VMEM((heads, 1, entries), F32),
             pltpu.VMEM((3 * width, wide), BF16),
             pltpu.VMEM((width, wide), BF16),
-            pltpu.VMEM((tp, wide, width), BF16),
-            pltpu.VMEM((tp, width, width), BF16),
+            pltpu.VMEM((tp * hidden, wide), BF16),
+            pltpu.VMEM((tp * hidden, width), BF16),
             pltpu.VMEM((micro, cells, width), BF16),
             pltpu.VMEM((micro, 2, cells, width), BF16),
             pltpu.VMEM((micro, cells, width), BF16),
@@ -363,6 +370,7 @@
             pltpu.VMEM((cells, wide), BF16),
             pltpu.VMEM((lines, lanes), F32),
             pltpu.VMEM((heads * half_cells, 2 * half_cells), F32),
+            pltpu.VMEM((2 * half_cells, heads * half_cells), F32),
             dma((14,)),
             dma((4, 3)),
             dma((4, 3)),

time: 37.5 us -> 38.5 us (1.027)
  the two profiles are of different devices: /device:TPU:11 before, /device:TPU:19 now
where the time goes in v3:
time: 38.5 us; the launch traced here: 38 us
  Pallas kernels  36.3 us (94%)
  local copies, waits for them, and re-layouts  1.69 us (4%)
    pallas_call x1, Pallas kernels, on_device(): pl.pallas_call(functools.partial(kernel, tp, micro, heads, slabs, edges),...  36.3 us
    unnamed x1, local copies, waits for them, and re-layouts  1.69 us

profile of v3, /device:TPU:19, one launch (start us, length us, event | category | flops | bytes accessed | tf_op | source)
XLA Modules:
  0.0 38.0 jit_solution(9287335969614781049)
XLA Ops:
  0.0 36.3 %shard_map.136 = bf16[2,288,192]{2,1,0:T(8,128)(2,1)} custom-call(bf16[2,288,192]{2,1,0:T(8,128)(2,1)} %bitcast.12, bf16[1,192]{1,0:T(2,128)(2,1)} %g1_in.1, bf16[1,192]{1,0:T(2,128)(2,1)} %s1_in.1, bf16[144,192]{1,0:T(8,128)(2,1)} %bitcast.15, bf16[1,144]{1,0:T(2,128)(2,1)} %qb_in.1, bf16[48,192]{1,0:T(8,128)(2,1)} %bitcast.17, bf16[1,48]{1,0:T(2,128)(2,1)} %pb_in.1, ...), custom_call_target="tpu_custom_call" | custom-call | tf_op jit(solution)/shard_map/pallas_call | solution.py:340
  36.3 1.7 %copy.16 = bf16[1,2,2,3,48,192]{5,4,3,2,1,0:T(8,128)(2,1)} copy(bf16[1,2,2,3,48,192]{5,4,3,2,1,0:T(8,128)(2,1)} %bitcast.11) | data formatting | bytes 442368

commit v4 on v3

--- a/solution.py
+++ b/solution.py
@@ -167,13 +167,6 @@
     near_n[...] = ones
     att_n[...] = ones
 
-    @pl.when(section == 0)
-    def _():
-        for t in range(micro):
-            inbuf[t, 0] = mm(perm[...], x_ref[t]).astype(BF16)
-
-    hand_on(0)
-
     table[...] = jnp.zeros_like(table)
     span = WH * (2 * WW - 1)
     for zq in range(WZ):
@@ -196,18 +189,18 @@
     pick = (lax.broadcasted_iota(jnp.int32, (table.shape[1], 2 * half_cells), 0) == place).astype(F32).astype(BF16)
     full = table[...]
     lines = full.shape[0]
+    turned = jnp.concatenate(
+        [full if wq == 0 else pltpu.roll(full, full.shape[1] - wq, 1) for wq in range(WW)], axis=0)
+    first = turned.astype(BF16)
+    rest = turned - first.astype(F32)
+    second = rest.astype(BF16)
+    third = (rest - second.astype(F32)).astype(BF16)
+    hand_on(0)
+    total = mm(first, pick) + mm(second, pick) + mm(third, pick)
     for wq in range(WW):
-        turned = full if wq == 0 else pltpu.roll(full, full.shape[1] - wq, 1)
-        first = turned.astype(BF16)
-        rest = turned - first.astype(F32)
-        second = rest.astype(BF16)
-        third = (rest - second.astype(F32)).astype(BF16)
-        parts = mm(
-            jnp.concatenate([p.astype(F32) for p in (first, second, third)], axis=0).astype(BF16), pick)
-        total = parts[:lines] + parts[lines:2 * lines] + parts[2 * lines:]
         for h in range(heads):
-            at = h * half_cells + wq * GROUP
-            spread[at:at + GROUP, :] = total[h * GROUP:(h + 1) * GROUP]
+            at, row = h * half_cells + wq * GROUP, wq * lines + h * GROUP
+            spread[at:at + GROUP, :] = total[row:row + GROUP]
     bias[...] = spread[...].T * LOG2E
 
     hand_on(1)
@@ -215,8 +208,6 @@
     @pl.when(section == 0)
     def _():
         field_copy().wait_recv()
-        for t in range(micro):
-            inbuf[t, 1] = mm(perm[...], near[t]).astype(BF16)
 
     scale = LOG2E / float(np.sqrt(head_size))
     lane_head = lax.broadcasted_iota(jnp.int32, (half_cells, width), 1)
@@ -229,12 +220,19 @@
             weight_copy(kind, 2).wait_recv()
 
     def turn(t, carry):
+        @pl.when(section == 0)
+        def _():
+            inbuf[t, 0] = mm(perm[...], x_ref[t]).astype(BF16)
+            inbuf[t, 1] = mm(perm[...], near[t]).astype(BF16)
+
         @pl.when(section == 1)
         def _():
             for part in range(chunks):
                 state_copy(t, 0, part).wait_recv()
                 if part < chunks - 1:
-                    state_forward(t, part).start()
+                    @pl.when(t == 0)
+                    def _():
+                        state_forward(t, part).start()
 
         g1, s1 = g1_ref[...].astype(F32), s1_ref[...].astype(F32)
         g2, s2 = g2_ref[...].astype(F32), s2_ref[...].astype(F32)
@@ -253,6 +251,11 @@
         near_n[:, :width] = layer_norm(inbuf[t, 1].astype(F32), g1, s1).astype(BF16)
         k_near = mm_nt(near_n[...], qkv[width:2 * width, :])
         v_near = mm_nt(near_n[...], qkv[2 * width:, :])
+
+        @pl.when(t == 0)
+        def _():
+            hand_on(2)
+
         attended = []
         for s in range(slabs):
             cut = slice(s * half_cells, (s + 1) * half_cells)
@@ -267,11 +270,12 @@
             for h, m in enumerate(in_head):
                 total = jnp.where(m, mixed[h * half_cells:(h + 1) * half_cells], total)
             attended.append(total)
-            if s in (0, 2):
-                @pl.when(t == 0)
-                def _():
-                    hand_on(2 + s // 2)
         att_n[:, :width] = jnp.concatenate(attended, axis=0).astype(BF16)
+
+        @pl.when(t == 0)
+        def _():
+            hand_on(3)
+
         weights_here(t, 1)
         middle = (grid + mm_nt(att_n[...], proj[...])).astype(BF16).astype(F32)
         pick_row = (lax.broadcasted_iota(jnp.int32, (16, wide), 1) == width + 1).astype(F32).astype(BF16)
@@ -291,6 +295,10 @@
             def _():
                 state_copy(t, 0, part).start()
                 if part == chunks - 1:
+                    @pl.when(t > 0)
+                    def _():
+                        for early in range(chunks - 1):
+                            state_copy(t, 1, early).start()
                     state_copy(t, 1, part).start()
 
         out_ref[t] = mm(unperm[...], outp[t]).astype(BF16)
@@ -308,13 +316,13 @@
         for t in range(micro):
             for part in range(chunks):
                 state_copy(t, 0, part).wait_send()
-            state_copy(t, 1, chunks - 1).wait_send()
+                if t > 0 or part == chunks - 1:
+                    state_copy(t, 1, part).wait_send()
 
     @pl.when(section == 1)
     def _():
-        for t in range(micro):
-            for part in range(chunks - 1):
-                state_forward(t, part).wait_send()
+        for part in range(chunks - 1):
+            state_forward(0, part).wait_send()
 
 
 def on_device(

time: 38.5 us -> 33.9 us (0.88)
  Pallas kernels: 36.3 us -> 32 us
    pallas_call x1, Pallas kernels: 36.3 us -> 32 us  [on_device(): pl.pallas_call(functools.partial(kernel, tp, micro, heads, slabs, edges),...]
where the time goes in v4:
time: 33.9 us; the launch traced here: 33.7 us
  Pallas kernels  32 us (94%)
  local copies, waits for them, and re-layouts  1.69 us (5%)
    pallas_call x1, Pallas kernels, on_device(): pl.pallas_call(functools.partial(kernel, tp, micro, heads, slabs, edges),...  32 us
    unnamed x1, local copies, waits for them, and re-layouts  1.69 us

profile of v4, /device:TPU:19, one launch (start us, length us, event | category | flops | bytes accessed | tf_op | source)
XLA Modules:
  0.0 33.7 jit_solution(8859390795662791008)
XLA Ops:
  0.0 32.0 %shard_map.136 = bf16[2,288,192]{2,1,0:T(8,128)(2,1)} custom-call(bf16[2,288,192]{2,1,0:T(8,128)(2,1)} %bitcast.12, bf16[1,192]{1,0:T(2,128)(2,1)} %g1_in.1, bf16[1,192]{1,0:T(2,128)(2,1)} %s1_in.1, bf16[144,192]{1,0:T(8,128)(2,1)} %bitcast.15, bf16[1,144]{1,0:T(2,128)(2,1)} %qb_in.1, bf16[48,192]{1,0:T(8,128)(2,1)} %bitcast.17, bf16[1,48]{1,0:T(2,128)(2,1)} %pb_in.1, ...), custom_call_target="tpu_custom_call" | custom-call | tf_op jit(solution)/shard_map/pallas_call | solution.py:348
  32.0 1.7 %copy.16 = bf16[1,2,2,3,48,192]{5,4,3,2,1,0:T(8,128)(2,1)} copy(bf16[1,2,2,3,48,192]{5,4,3,2,1,0:T(8,128)(2,1)} %bitcast.11) | data formatting | bytes 442368

commit v5 on v3

v5 whole, which is shorter than its diff:
```python
import functools

import jax
import jax.numpy as jnp
import numpy as np
from jax import lax
from jax.experimental import pallas as pl
from jax.experimental.pallas import tpu as pltpu
from jax.sharding import PartitionSpec as P

WZ = 2
WH = 6
WW = 12
HALF = WH // 2
GROUP = WZ * HALF
EPS = 1e-05
MESH = pl.DeviceIdType.MESH
F32 = jnp.float32
BF16 = jnp.bfloat16
NT = (((1,), (1,)), ((), ()))
TN = (((0,), (0,)), ((), ()))
LOG2E = float(np.log2(np.e))


def mm(a, b):
    return jnp.dot(a, b, preferred_element_type=F32)


def mm_nt(a, b):
    return lax.dot_general(a, b, NT, preferred_element_type=F32)


def layer_norm(values, gain, shift):
    mean = jnp.mean(values, axis=-1, keepdims=True)
    centred = values - mean
    spread = jnp.mean(centred * centred, axis=-1, keepdims=True)
    return centred * lax.rsqrt(spread + EPS) * gain + shift


def kernel(
    tp, heads, slabs, edges,
    x_in, g1_in, s1_in, qw_in, qb_in, pw_in, pb_in, g2_in, s2_in,
    ew_in, eb_in, rw_in, rb_in, table_in,
    out_ref,
    x_ref, g1_ref, s1_ref, qw_ref, qb_ref, pw_ref, pb_ref, g2_ref, s2_ref,
    ew_ref, eb_ref, rb_ref, tables,
    qkv, proj, expand, reduce, norms, near_raw, near_mid, outp, foreign, perm, unperm,
    own_n, near_n, att_n, table, spread, bias,
    l_sem, w_send, w_recv, f_send, f_recv, n_send, n_recv, o_send, o_recv,
):
    me = lax.axis_index("tp")
    lat = lax.axis_index("lat")
    section = lax.axis_index("section")
    pair = lat + 1 - 2 * lax.rem(lat, 2)
    other = 1 - section
    cells, width = x_ref.shape
    wide = own_n.shape[1]
    half_cells = cells // slabs
    head_size = width // heads
    q_part, p_part, e_part = qw_ref.shape[0], pw_ref.shape[0], ew_ref.shape[1]
    core_peer = me + 1 - 2 * lax.rem(me, 2)
    chip_peer = lax.rem(me + tp // 2, tp)

    barrier = pltpu.get_barrier_semaphore()
    pl.semaphore_signal(barrier, inc=1, device_id={"tp": core_peer}, device_id_type=MESH)
    pl.semaphore_signal(barrier, inc=1, device_id={"tp": chip_peer}, device_id_type=MESH)
    pl.semaphore_signal(barrier, inc=1, device_id={"lat": pair}, device_id_type=MESH)
    pl.semaphore_signal(barrier, inc=1, device_id={"section": other}, device_id_type=MESH)

    def owner_rows(owner, part):
        return pl.ds(pl.multiple_of(owner * part, 16), part)

    loads = [
        pltpu.make_async_copy(source, target, l_sem.at[n])
        for n, (source, target) in enumerate((
            (qw_in, qw_ref), (qb_in, qb_ref), (pw_in, pw_ref), (pb_in, pb_ref), (rb_in, rb_ref),
            (ew_in, ew_ref), (eb_in, eb_ref), (rw_in, reduce.at[section, owner_rows(me, e_part), :]),
            (g1_in, g1_ref), (s1_in, s1_ref), (g2_in, g2_ref), (s2_in, s2_ref),
            (x_in.at[section], x_ref), (table_in, tables.at[section]),
        ))
    ]
    for load in loads:
        load.start()

    for load in loads[:5]:
        load.wait()
    tail = lax.broadcasted_iota(jnp.int32, (wide - width, q_part), 0)
    q_tail = jnp.where(tail == 0, qb_ref[...].astype(F32), 0.0).T
    qkv[section, owner_rows(me, q_part), :] = jnp.concatenate(
        [qw_ref[...].astype(F32), q_tail], axis=1).astype(BF16)
    tail = lax.broadcasted_iota(jnp.int32, (wide - width, p_part), 0)
    p_tail = jnp.where(
        tail == 0, pb_ref[...].astype(F32), jnp.where(tail == 1, rb_ref[...].astype(F32), 0.0)).T
    proj[section, owner_rows(me, p_part), :] = jnp.concatenate(
        [pw_ref[...].astype(F32), p_tail], axis=1).astype(BF16)
    for load in loads[5:12]:
        load.wait()
    tail = lax.broadcasted_iota(jnp.int32, (wide - width, e_part), 0)
    expand[section, owner_rows(me, e_part), :] = jnp.concatenate(
        [ew_ref[...].astype(F32), jnp.where(tail == 0, eb_ref[...].astype(F32), 0.0)], axis=0).T.astype(BF16)
    line = lax.broadcasted_iota(jnp.int32, (16, width), 0)
    packed = jnp.where(line == 0, g1_ref[...].astype(F32), s1_ref[...].astype(F32))
    packed = jnp.where(line == 2, g2_ref[...].astype(F32), packed)
    norms[section] = jnp.where(line == 3, s2_ref[...].astype(F32), packed).astype(BF16)

    pl.semaphore_wait(barrier, 4)

    def weight_copy(model, kind, way):
        owner = chip_peer if way == 2 else me
        target = (
            lambda: qkv.at[model, owner_rows(owner, q_part), :],
            lambda: proj.at[model, owner_rows(owner, p_part), :],
            lambda: expand.at[model, owner_rows(owner, e_part), :],
            lambda: reduce.at[model, owner_rows(owner, e_part), :],
            lambda: norms.at[model],
            lambda: tables.at[model],
        )[kind]()
        device = ({"tp": core_peer}, {"tp": chip_peer}, {"tp": core_peer}, {"section": other})[way]
        return pltpu.make_async_remote_copy(
            src_ref=table_in if kind == 5 else target, dst_ref=target,
            send_sem=w_send.at[model, kind, way], recv_sem=w_recv.at[model, kind, way],
            device_id=device, device_id_type=MESH)

    def share_out(model, kind):
        @pl.when(section != model)
        def _():
            weight_copy(model, kind, 3).wait_recv()

        weight_copy(model, kind, 1).start()
        weight_copy(model, kind, 0).start()

    def hand_on(model, kind):
        weight_copy(model, kind, 1).wait_recv()
        weight_copy(model, kind, 2).start()

    def weights_here(model, kind):
        weight_copy(model, kind, 0).wait_recv()
        weight_copy(model, kind, 2).wait_recv()

    field_copy = pltpu.make_async_remote_copy(
        src_ref=x_in.at[section], dst_ref=near_raw, send_sem=f_send, recv_sem=f_recv,
        device_id={"lat": pair}, device_id_type=MESH)
    chunks = len(edges) - 1

    def pair_copy(part):
        rows = pl.ds(edges[part], edges[part + 1] - edges[part])
        return pltpu.make_async_remote_copy(
            src_ref=outp.at[0, rows], dst_ref=near_mid.at[rows], send_sem=n_send.at[part],
            recv_sem=n_recv.at[part], device_id={"lat": pair}, device_id_type=MESH)

    def result_copy(model, part):
        rows = pl.ds(edges[part], edges[part + 1] - edges[part])
        return pltpu.make_async_remote_copy(
            src_ref=outp.at[model, rows], dst_ref=foreign.at[rows], send_sem=o_send.at[part],
            recv_sem=o_recv.at[part], device_id={"section": other}, device_id_type=MESH)

    weight_copy(section, 0, 3).start()

    @pl.when(section == 0)
    def _():
        weight_copy(0, 0, 1).start()
        weight_copy(0, 0, 0).start()

    field_copy.start()
    for kind in (5, 4, 1, 2, 3):
        weight_copy(section, kind, 3).start()

    @pl.when(section == 0)
    def _():
        for kind in (1, 2, 3):
            weight_copy(0, kind, 1).start()
            weight_copy(0, kind, 0).start()

    def share_on(kind):
        @pl.when(section == 1)
        def _():
            weight_copy(0, kind, 3).wait_recv()
            weight_copy(0, kind, 1).start()
            weight_copy(0, kind, 0).start()

    for load in loads[12:]:
        load.wait()

    stretch = cells // GROUP
    step = -(-65536 // GROUP)
    line = lax.broadcasted_iota(jnp.int32, (1, cells), 1)
    level_row = sum((line >= stretch * k).astype(jnp.int32) for k in range(1, GROUP))
    forth = (line - stretch * level_row) * GROUP + level_row
    column = lax.shift_right_logical(line * step, 16)
    back = (line - GROUP * column) * stretch + column
    rows = lax.broadcasted_iota(jnp.int32, (cells, cells), 0)
    perm[...] = (rows == forth).astype(F32).astype(BF16)
    unperm[...] = (rows == back).astype(F32).astype(BF16)
    lanes = lax.broadcasted_iota(jnp.int32, (cells, wide), 1)
    ones = (lanes == width).astype(F32).astype(BF16)
    own_n[...] = ones
    near_n[...] = ones
    att_n[...] = ones
    own_field = mm(perm[...], x_ref[...])

    span = WH * (2 * WW - 1)
    c = lax.broadcasted_iota(jnp.int32, (1, 2 * half_cells), 1)
    far = (c >= half_cells).astype(jnp.int32)
    c = c - half_cells * far
    wk = sum((c >= GROUP * k).astype(jnp.int32) for k in range(1, WW))
    zr = c - GROUP * wk
    zk = (zr >= HALF).astype(jnp.int32)
    band = lax.rem(lat, 2)
    hk = zr - HALF * zk + HALF * (band + far - 2 * band * far)
    place = zk * span + hk * (2 * WW - 1) + WW - 1 - wk
    pick = (lax.broadcasted_iota(jnp.int32, (table.shape[1], 2 * half_cells), 0) == place).astype(F32).astype(BF16)
    table[...] = jnp.zeros_like(table)

    def expand_bias(model):
        for zq in range(WZ):
            for zk in range(WZ):
                for r in range(HALF):
                    off = ((zq * WZ + zk) * HALF + r) * span
                    piece = tables[model, :, 0, off:off + span]
                    for h in range(heads):
                        row = h * GROUP + zq * HALF + r
                        table[row:row + 1, zk * span:(zk + 1) * span] = piece[h:h + 1]
        full = table[...]
        lines = full.shape[0]
        turned = jnp.concatenate(
            [full if wq == 0 else pltpu.roll(full, full.shape[1] - wq, 1) for wq in range(WW)], axis=0)
        first = turned.astype(BF16)
        rest = turned - first.astype(F32)
        second = rest.astype(BF16)
        third = (rest - second.astype(F32)).astype(BF16)
        total = mm(first, pick) + mm(second, pick) + mm(third, pick)
        for wq in range(WW):
            for h in range(heads):
                at, row = h * half_cells + wq * GROUP, wq * lines + h * GROUP
                spread[at:at + GROUP, :] = total[row:row + GROUP]
        bias[...] = spread[...].T * LOG2E

    share_on(0)
    share_on(1)

    scale = LOG2E / float(np.sqrt(head_size))
    lane_head = lax.broadcasted_iota(jnp.int32, (half_cells, width), 1)
    in_head = [(lane_head >= h * head_size) & (lane_head < (h + 1) * head_size) for h in range(heads)]

    for model in range(2):
        @pl.when(section != model)
        def _():
            weight_copy(model, 4, 3).wait_recv()
            weight_copy(model, 5, 3).wait_recv()

        expand_bias(model)
        g1, s1, g2, s2 = (norms[model, n:n + 1, :].astype(F32) for n in range(4))
        hand_on(model, 0)
        grid = own_field if model == 0 else outp[0].astype(F32)
        own_n[:, :width] = layer_norm(grid, g1, s1).astype(BF16)
        if model == 0:
            share_on(2)
        hand_on(model, 1)
        weights_here(model, 0)
        q = mm_nt(own_n[...], qkv[model, :width, :])
        k_own = mm_nt(own_n[...], qkv[model, width:2 * width, :])
        v_own = mm_nt(own_n[...], qkv[model, 2 * width:, :])
        if model == 0:
            field_copy.wait_recv()
            near = mm(perm[...], near_raw[...])
        else:
            for part in range(chunks):
                pair_copy(part).wait_recv()
            near = near_mid[...].astype(F32)
        near_n[:, :width] = layer_norm(near, g1, s1).astype(BF16)
        k_near = mm_nt(near_n[...], qkv[model, width:2 * width, :])
        v_near = mm_nt(near_n[...], qkv[model, 2 * width:, :])
        if model == 0:
            share_on(3)
        attended = []
        for s in range(slabs):
            cut = slice(s * half_cells, (s + 1) * half_cells)
            keys = jnp.concatenate([k_own[cut], k_near[cut]], axis=0).astype(BF16)
            vals = jnp.concatenate([v_own[cut], v_near[cut]], axis=0).astype(BF16)
            stack = jnp.concatenate([jnp.where(m, q[cut], 0.0) for m in in_head], axis=0).astype(BF16)
            scores = mm_nt(keys, stack) * scale + bias[...]
            e = jnp.exp2(scores - jnp.max(scores, axis=0, keepdims=True))
            probs = (e * (1.0 / jnp.sum(e, axis=0, keepdims=True))).astype(BF16)
            mixed = lax.dot_general(probs, vals, TN, preferred_element_type=F32)
            total = jnp.zeros((half_cells, width), F32)
            for h, m in enumerate(in_head):
                total = jnp.where(m, mixed[h * half_cells:(h + 1) * half_cells], total)
            attended.append(total)
        att_n[:, :width] = jnp.concatenate(attended, axis=0).astype(BF16)
        hand_on(model, 2)
        hand_on(model, 3)
        weights_here(model, 1)
        middle = (grid + mm_nt(att_n[...], proj[model])).astype(BF16).astype(F32)
        pick_row = (lax.broadcasted_iota(jnp.int32, (16, wide), 1) == width + 1).astype(F32).astype(BF16)
        shift_out = mm_nt(pick_row, proj[model])[:1]
        own_n[:, :width] = layer_norm(middle, g2, s2).astype(BF16)
        if model == 0:
            for kind in range(4):
                share_out(1, kind)
        weights_here(model, 2)
        for part in range(chunks):
            cut = slice(edges[part], edges[part + 1])
            pre = mm_nt(own_n[cut, :], expand[model])
            hidden = (0.5 * pre * (1.0 + lax.erf(pre * float(np.sqrt(0.5))))).astype(BF16)
            if part == 0:
                weights_here(model, 3)
            result = middle[cut] + shift_out + mm(hidden, reduce[model])
            outp[model, cut, :] = result.astype(BF16)
            if model == 0:
                pair_copy(part).start()

            @pl.when(section != model)
            def _():
                result_copy(model, part).start()

    @pl.when(section == 0)
    def _():
        out_ref[0] = mm(unperm[...], outp[0]).astype(BF16)

    @pl.when(section == 1)
    def _():
        out_ref[1] = mm(unperm[...], outp[1]).astype(BF16)

    for part in range(chunks):
        result_copy(other, part).wait_recv()
    out_ref[other] = mm(unperm[...], foreign[...]).astype(BF16)

    for kind in range(6):
        weight_copy(section, kind, 3).wait_send()
    for model in range(2):
        for kind in range(4):
            for way in range(3):
                weight_copy(model, kind, way).wait_send()
    field_copy.wait_send()
    for part in range(chunks):
        pair_copy(part).wait_send()
        result_copy(other, part).wait_send()


def on_device(
    initial_field, first_gain, first_shift, qkv_weight, qkv_bias, proj_weight, proj_bias,
    second_gain, second_shift, expand_weight, expand_bias, reduce_weight, reduce_bias, earth_bias,
):
    tp = lax.axis_size("tp")
    micro, levels, lat_rows, lon, width = initial_field.shape
    cells = levels * lat_rows * lon
    heads, entries = earth_bias.shape[-2:]
    slabs = lon // WW
    half_cells = cells // slabs
    hidden = expand_weight.shape[2]
    wide = -(-(width + 2) // 128) * 128
    lines = -(-heads * GROUP // 8) * 8
    tiles = cells // 16
    edges = (0, tiles // 2 * 16, (tiles - tiles // 6) * 16, cells)
    chunks = len(edges) - 1
    lanes = -(-WZ * WH * (2 * WW - 1) // 128) * 128
    q_weight, p_weight = qkv_weight[0].T, proj_weight[0].T
    vmem = pl.BlockSpec(memory_space=pltpu.VMEM)
    dma = pltpu.SemaphoreType.DMA
    out = pl.pallas_call(
        functools.partial(kernel, tp, heads, slabs, edges),
        out_shape=jax.ShapeDtypeStruct((micro, cells, width), BF16),
        in_specs=[pl.BlockSpec(memory_space=pltpu.HBM)] * 14,
        out_specs=vmem,
        scratch_shapes=[
            pltpu.VMEM((cells, width), BF16),
            pltpu.VMEM((1, width), BF16),
            pltpu.VMEM((1, width), BF16),
            pltpu.VMEM(q_weight.shape, BF16),
            pltpu.VMEM(qkv_bias.shape, BF16),
            pltpu.VMEM(p_weight.shape, BF16),
            pltpu.VMEM(proj_bias.shape, BF16),
            pltpu.VMEM((1, width), BF16),
            pltpu.VMEM((1, width), BF16),
            pltpu.VMEM((width, hidden), BF16),
            pltpu.VMEM((1, hidden), BF16),
            pltpu.VMEM(reduce_bias.shape, BF16),
            pltpu.VMEM((2, heads, 1, entries), F32),
            pltpu.VMEM((2, 3 * width, wide), BF16),
            pltpu.VMEM((2, width, wide), BF16),
            pltpu.VMEM((2, tp * hidden, wide), BF16),
            pltpu.VMEM((2, tp * hidden, width), BF16),
            pltpu.VMEM((2, 16, width), BF16),
            pltpu.VMEM((cells, width), BF16),
            pltpu.VMEM((cells, width), BF16),
            pltpu.VMEM((2, cells, width), BF16),
            pltpu.VMEM((cells, width), BF16),
            pltpu.VMEM((cells, cells), BF16),
            pltpu.VMEM((cells, cells), BF16),
            pltpu.VMEM((cells, wide), BF16),
            pltpu.VMEM((cells, wide), BF16),
            pltpu.VMEM((cells, wide), BF16),
            pltpu.VMEM((lines, lanes), F32),
            pltpu.VMEM((heads * half_cells, 2 * half_cells), F32),
            pltpu.VMEM((2 * half_cells, heads * half_cells), F32),
            dma((14,)),
            dma((2, 6, 4)),
            dma((2, 6, 4)),
            dma,
            dma,
            dma((chunks,)),
            dma((chunks,)),
            dma((chunks,)),
            dma((chunks,)),
        ],
        compiler_params=pltpu.CompilerParams(
            collective_id=0, has_side_effects=True, vmem_limit_bytes=60 * 1024 * 1024),
    )(
        initial_field.reshape(micro, cells, width), first_gain, first_shift, q_weight, qkv_bias,
        p_weight, proj_bias, second_gain, second_shift, expand_weight[0], expand_bias,
        reduce_weight[0], reduce_bias, earth_bias.reshape(heads, 1, entries),
    )
    return out.reshape(1, micro, levels, lat_rows, lon, width)


def solution(mesh):
    return jax.shard_map(
        on_device,
        mesh=mesh,
        in_specs=(
            P(None, "tp", "lat", None, None),
            P("section", None),
            P("section", None),
            P("section", None, "tp"),
            P("section", "tp"),
            P("section", None, "tp"),
            P("section", "tp"),
            P("section", None),
            P("section", None),
            P("section", None, "tp"),
            P("section", "tp"),
            P("section", "tp", None),
            P("section", "tp"),
            P("section", "tp", "lat", None, None),
        ),
        out_specs=P("section", None, "tp", "lat", None, None),
        check_vma=False,
    )
```

time: 38.5 us -> 30.9 us (0.80)
  Pallas kernels: 36.3 us -> 29 us
    pallas_call x1, Pallas kernels: 36.3 us -> 29 us  [on_device(): pl.pallas_call(functools.partial(kernel, tp, heads, slabs, edges), out_sh...]
where the time goes in v5:
time: 30.9 us; the launch traced here: 30.7 us
  Pallas kernels  29 us (94%)
  local copies, waits for them, and re-layouts  1.69 us (5%)
    pallas_call x1, Pallas kernels, on_device(): pl.pallas_call(functools.partial(kernel, tp, heads, slabs, edges), out_sh...  29 us
    unnamed x1, local copies, waits for them, and re-layouts  1.69 us

profile of v5, /device:TPU:19, one launch (start us, length us, event | category | flops | bytes accessed | tf_op | source)
XLA Modules:
  0.0 30.7 jit_solution(5511329255024967655)
XLA Ops:
  0.0 29.0 %shard_map.136 = bf16[2,288,192]{2,1,0:T(8,128)(2,1)} custom-call(bf16[2,288,192]{2,1,0:T(8,128)(2,1)} %bitcast.12, bf16[1,192]{1,0:T(2,128)(2,1)} %g1_in.1, bf16[1,192]{1,0:T(2,128)(2,1)} %s1_in.1, bf16[144,192]{1,0:T(8,128)(2,1)} %bitcast.15, bf16[1,144]{1,0:T(2,128)(2,1)} %qb_in.1, bf16[48,192]{1,0:T(8,128)(2,1)} %bitcast.17, bf16[1,48]{1,0:T(2,128)(2,1)} %pb_in.1, ...), custom_call_target="tpu_custom_call" | custom-call | tf_op jit(solution)/shard_map/pallas_call | solution.py:360
  29.0 1.7 %copy.16 = bf16[1,2,2,3,48,192]{5,4,3,2,1,0:T(8,128)(2,1)} copy(bf16[1,2,2,3,48,192]{5,4,3,2,1,0:T(8,128)(2,1)} %bitcast.11) | data formatting | bytes 442368

commit v6 on v5

--- a/solution.py
+++ b/solution.py
@@ -82,12 +82,80 @@
     for load in loads:
         load.start()
 
-    for load in loads[:5]:
+    for load in loads[:2]:
         load.wait()
     tail = lax.broadcasted_iota(jnp.int32, (wide - width, q_part), 0)
     q_tail = jnp.where(tail == 0, qb_ref[...].astype(F32), 0.0).T
     qkv[section, owner_rows(me, q_part), :] = jnp.concatenate(
         [qw_ref[...].astype(F32), q_tail], axis=1).astype(BF16)
+    pl.semaphore_wait(barrier, 4)
+
+    def weight_copy(model, kind, way):
+        owner = chip_peer if way == 2 else me
+        target = (
+            lambda: qkv.at[model, owner_rows(owner, q_part), :],
+            lambda: proj.at[model, owner_rows(owner, p_part), :],
+            lambda: expand.at[model, owner_rows(owner * 2, e_part // 2), :],
+            lambda: expand.at[model, owner_rows(owner * 2 + 1, e_part // 2), :],
+            lambda: reduce.at[model, owner_rows(owner * 2, e_part // 2), :],
+            lambda: reduce.at[model, owner_rows(owner * 2 + 1, e_part // 2), :],
+            lambda: norms.at[model],
+            lambda: tables.at[model],
+        )[kind]()
+        device = ({"tp": core_peer}, {"tp": chip_peer}, {"tp": core_peer}, {"section": other})[way]
+        return pltpu.make_async_remote_copy(
+            src_ref=table_in if kind == 7 else target, dst_ref=target,
+            send_sem=w_send.at[model, kind, way], recv_sem=w_recv.at[model, kind, way],
+            device_id=device, device_id_type=MESH)
+
+    def share_out(model, kind):
+        @pl.when(section != model)
+        def _():
+            weight_copy(model, kind, 3).wait_recv()
+
+        weight_copy(model, kind, 1).start()
+        weight_copy(model, kind, 0).start()
+
+    def hand_on(model, kind):
+        weight_copy(model, kind, 1).wait_recv()
+        weight_copy(model, kind, 2).start()
+
+    def weights_here(model, kind):
+        weight_copy(model, kind, 0).wait_recv()
+        weight_copy(model, kind, 2).wait_recv()
+
+    field_copy = pltpu.make_async_remote_copy(
+        src_ref=x_in.at[section], dst_ref=near_raw, send_sem=f_send, recv_sem=f_recv,
+        device_id={"lat": pair}, device_id_type=MESH)
+    chunks = len(edges) - 1
+
+    def pair_copy(part):
+        rows = pl.ds(edges[part], edges[part + 1] - edges[part])
+        return pltpu.make_async_remote_copy(
+            src_ref=outp.at[0, rows], dst_ref=near_mid.at[rows], send_sem=n_send.at[part],
+            recv_sem=n_recv.at[part], device_id={"lat": pair}, device_id_type=MESH)
+
+    def result_copy(model, part):
+        rows = pl.ds(edges[part], edges[part + 1] - edges[part])
+        return pltpu.make_async_remote_copy(
+            src_ref=outp.at[model, rows], dst_ref=foreign.at[rows], send_sem=o_send.at[part],
+            recv_sem=o_recv.at[part], device_id={"section": other}, device_id_type=MESH)
+
+    def own_shares(*kinds):
+        for kind in kinds:
+            weight_copy(section, kind, 3).start()
+
+        @pl.when(section == 0)
+        def _():
+            for kind in kinds:
+                if kind < 6:
+                    weight_copy(0, kind, 1).start()
+                    weight_copy(0, kind, 0).start()
+
+    own_shares(0, 7)
+    field_copy.start()
+    for load in loads[2:5]:
+        load.wait()
     tail = lax.broadcasted_iota(jnp.int32, (wide - width, p_part), 0)
     p_tail = jnp.where(
         tail == 0, pb_ref[...].astype(F32), jnp.where(tail == 1, rb_ref[...].astype(F32), 0.0)).T
@@ -95,81 +163,15 @@
         [pw_ref[...].astype(F32), p_tail], axis=1).astype(BF16)
     for load in loads[5:12]:
         load.wait()
-    tail = lax.broadcasted_iota(jnp.int32, (wide - width, e_part), 0)
-    expand[section, owner_rows(me, e_part), :] = jnp.concatenate(
-        [ew_ref[...].astype(F32), jnp.where(tail == 0, eb_ref[...].astype(F32), 0.0)], axis=0).T.astype(BF16)
     line = lax.broadcasted_iota(jnp.int32, (16, width), 0)
     packed = jnp.where(line == 0, g1_ref[...].astype(F32), s1_ref[...].astype(F32))
     packed = jnp.where(line == 2, g2_ref[...].astype(F32), packed)
     norms[section] = jnp.where(line == 3, s2_ref[...].astype(F32), packed).astype(BF16)
-
-    pl.semaphore_wait(barrier, 4)
-
-    def weight_copy(model, kind, way):
-        owner = chip_peer if way == 2 else me
-        target = (
-            lambda: qkv.at[model, owner_rows(owner, q_part), :],
-            lambda: proj.at[model, owner_rows(owner, p_part), :],
-            lambda: expand.at[model, owner_rows(owner, e_part), :],
-            lambda: reduce.at[model, owner_rows(owner, e_part), :],
-            lambda: norms.at[model],
-            lambda: tables.at[model],
-        )[kind]()
-        device = ({"tp": core_peer}, {"tp": chip_peer}, {"tp": core_peer}, {"section": other})[way]
-        return pltpu.make_async_remote_copy(
-            src_ref=table_in if kind == 5 else target, dst_ref=target,
-            send_sem=w_send.at[model, kind, way], recv_sem=w_recv.at[model, kind, way],
-            device_id=device, device_id_type=MESH)
-
-    def share_out(model, kind):
-        @pl.when(section != model)
-        def _():
-            weight_copy(model, kind, 3).wait_recv()
-
-        weight_copy(model, kind, 1).start()
-        weight_copy(model, kind, 0).start()
-
-    def hand_on(model, kind):
-        weight_copy(model, kind, 1).wait_recv()
-        weight_copy(model, kind, 2).start()
-
-    def weights_here(model, kind):
-        weight_copy(model, kind, 0).wait_recv()
-        weight_copy(model, kind, 2).wait_recv()
-
-    field_copy = pltpu.make_async_remote_copy(
-        src_ref=x_in.at[section], dst_ref=near_raw, send_sem=f_send, recv_sem=f_recv,
-        device_id={"lat": pair}, device_id_type=MESH)
-    chunks = len(edges) - 1
-
-    def pair_copy(part):
-        rows = pl.ds(edges[part], edges[part + 1] - edges[part])
-        return pltpu.make_async_remote_copy(
-            src_ref=outp.at[0, rows], dst_ref=near_mid.at[rows], send_sem=n_send.at[part],
-            recv_sem=n_recv.at[part], device_id={"lat": pair}, device_id_type=MESH)
-
-    def result_copy(model, part):
-        rows = pl.ds(edges[part], edges[part + 1] - edges[part])
-        return pltpu.make_async_remote_copy(
-            src_ref=outp.at[model, rows], dst_ref=foreign.at[rows], send_sem=o_send.at[part],
-            recv_sem=o_recv.at[part], device_id={"section": other}, device_id_type=MESH)
-
-    weight_copy(section, 0, 3).start()
-
-    @pl.when(section == 0)
-    def _():
-        weight_copy(0, 0, 1).start()
-        weight_copy(0, 0, 0).start()
-
-    field_copy.start()
-    for kind in (5, 4, 1, 2, 3):
-        weight_copy(section, kind, 3).start()
-
-    @pl.when(section == 0)
-    def _():
-        for kind in (1, 2, 3):
-            weight_copy(0, kind, 1).start()
-            weight_copy(0, kind, 0).start()
+    own_shares(6, 1)
+    tail = lax.broadcasted_iota(jnp.int32, (wide - width, e_part), 0)
+    expand[section, owner_rows(me, e_part), :] = jnp.concatenate(
+        [ew_ref[...].astype(F32), jnp.where(tail == 0, eb_ref[...].astype(F32), 0.0)], axis=0).T.astype(BF16)
+    own_shares(2, 3, 4, 5)
 
     def share_on(kind):
         @pl.when(section == 1)
@@ -245,8 +247,8 @@
     for model in range(2):
         @pl.when(section != model)
         def _():
-            weight_copy(model, 4, 3).wait_recv()
-            weight_copy(model, 5, 3).wait_recv()
+            weight_copy(model, 6, 3).wait_recv()
+            weight_copy(model, 7, 3).wait_recv()
 
         expand_bias(model)
         g1, s1, g2, s2 = (norms[model, n:n + 1, :].astype(F32) for n in range(4))
@@ -255,6 +257,7 @@
         own_n[:, :width] = layer_norm(grid, g1, s1).astype(BF16)
         if model == 0:
             share_on(2)
+            share_on(3)
         hand_on(model, 1)
         weights_here(model, 0)
         q = mm_nt(own_n[...], qkv[model, :width, :])
@@ -271,7 +274,8 @@
         k_near = mm_nt(near_n[...], qkv[model, width:2 * width, :])
         v_near = mm_nt(near_n[...], qkv[model, 2 * width:, :])
         if model == 0:
-            share_on(3)
+            share_on(4)
+            share_on(5)
         attended = []
         for s in range(slabs):
             cut = slice(s * half_cells, (s + 1) * half_cells)
@@ -288,22 +292,25 @@
             attended.append(total)
         att_n[:, :width] = jnp.concatenate(attended, axis=0).astype(BF16)
         hand_on(model, 2)
-        hand_on(model, 3)
         weights_here(model, 1)
         middle = (grid + mm_nt(att_n[...], proj[model])).astype(BF16).astype(F32)
         pick_row = (lax.broadcasted_iota(jnp.int32, (16, wide), 1) == width + 1).astype(F32).astype(BF16)
         shift_out = mm_nt(pick_row, proj[model])[:1]
         own_n[:, :width] = layer_norm(middle, g2, s2).astype(BF16)
+        for kind in (3, 4, 5):
+            hand_on(model, kind)
         if model == 0:
-            for kind in range(4):
+            for kind in range(6):
                 share_out(1, kind)
         weights_here(model, 2)
+        weights_here(model, 3)
         for part in range(chunks):
             cut = slice(edges[part], edges[part + 1])
             pre = mm_nt(own_n[cut, :], expand[model])
             hidden = (0.5 * pre * (1.0 + lax.erf(pre * float(np.sqrt(0.5))))).astype(BF16)
             if part == 0:
-                weights_here(model, 3)
+                weights_here(model, 4)
+                weights_here(model, 5)
             result = middle[cut] + shift_out + mm(hidden, reduce[model])
             outp[model, cut, :] = result.astype(BF16)
             if model == 0:
@@ -325,10 +332,10 @@
         result_copy(other, part).wait_recv()
     out_ref[other] = mm(unperm[...], foreign[...]).astype(BF16)
 
-    for kind in range(6):
+    for kind in range(8):
         weight_copy(section, kind, 3).wait_send()
     for model in range(2):
-        for kind in range(4):
+        for kind in range(6):
             for way in range(3):
                 weight_copy(model, kind, way).wait_send()
     field_copy.wait_send()
@@ -394,8 +401,8 @@
             pltpu.VMEM((heads * half_cells, 2 * half_cells), F32),
             pltpu.VMEM((2 * half_cells, heads * half_cells), F32),
             dma((14,)),
-            dma((2, 6, 4)),
-            dma((2, 6, 4)),
+            dma((2, 8, 4)),
+            dma((2, 8, 4)),
             dma,
             dma,
             dma((chunks,)),

time: 30.9 us -> 31.9 us (1.032); the launches traced: 30.7 us -> 31.3 us
  Pallas kernels: 29 us -> 29.6 us
    pallas_call x1, Pallas kernels: 29 us -> 29.6 us  [on_device(): pl.pallas_call(functools.partial(kernel, tp, heads, slabs, edges), out_sh...]
where the time goes in v6:
time: 31.9 us; the launch traced here: 31.3 us
  Pallas kernels  29.6 us (93%)
  local copies, waits for them, and re-layouts  1.69 us (5%)
    pallas_call x1, Pallas kernels, on_device(): pl.pallas_call(functools.partial(kernel, tp, heads, slabs, edges), out_sh...  29.6 us
    unnamed x1, local copies, waits for them, and re-layouts  1.69 us

profile of v6, /device:TPU:19, one launch (start us, length us, event | category | flops | bytes accessed | tf_op | source)
XLA Modules:
  0.0 31.3 jit_solution(8437488854931803984)
XLA Ops:
  0.0 29.6 %shard_map.136 = bf16[2,288,192]{2,1,0:T(8,128)(2,1)} custom-call(bf16[2,288,192]{2,1,0:T(8,128)(2,1)} %bitcast.12, bf16[1,192]{1,0:T(2,128)(2,1)} %g1_in.1, bf16[1,192]{1,0:T(2,128)(2,1)} %s1_in.1, bf16[144,192]{1,0:T(8,128)(2,1)} %bitcast.15, bf16[1,144]{1,0:T(2,128)(2,1)} %qb_in.1, bf16[48,192]{1,0:T(8,128)(2,1)} %bitcast.17, bf16[1,48]{1,0:T(2,128)(2,1)} %pb_in.1, ...), custom_call_target="tpu_custom_call" | custom-call | tf_op jit(solution)/shard_map/pallas_call | solution.py:367
  29.6 1.7 %copy.16 = bf16[1,2,2,3,48,192]{5,4,3,2,1,0:T(8,128)(2,1)} copy(bf16[1,2,2,3,48,192]{5,4,3,2,1,0:T(8,128)(2,1)} %bitcast.11) | data formatting | bytes 442368

commit v7 on v6

--- a/solution.py
+++ b/solution.py
@@ -38,13 +38,13 @@
 
 
 def kernel(
-    tp, heads, slabs, edges,
+    tp, heads, slabs, all_edges,
     x_in, g1_in, s1_in, qw_in, qb_in, pw_in, pb_in, g2_in, s2_in,
     ew_in, eb_in, rw_in, rb_in, table_in,
     out_ref,
     x_ref, g1_ref, s1_ref, qw_ref, qb_ref, pw_ref, pb_ref, g2_ref, s2_ref,
     ew_ref, eb_ref, rb_ref, tables,
-    qkv, proj, expand, reduce, norms, near_raw, near_mid, outp, foreign, perm, unperm,
+    first_share, second_share, reduce, near_raw, near_mid, outp, foreign, perm, unperm,
     own_n, near_n, att_n, table, spread, bias,
     l_sem, w_send, w_recv, f_send, f_recv, n_send, n_recv, o_send, o_recv,
 ):
@@ -82,29 +82,30 @@
     for load in loads:
         load.start()
 
-    for load in loads[:2]:
+    for load in loads[:2] + loads[8:12]:
         load.wait()
     tail = lax.broadcasted_iota(jnp.int32, (wide - width, q_part), 0)
     q_tail = jnp.where(tail == 0, qb_ref[...].astype(F32), 0.0).T
-    qkv[section, owner_rows(me, q_part), :] = jnp.concatenate(
+    first_share[section, me, :q_part, :] = jnp.concatenate(
         [qw_ref[...].astype(F32), q_tail], axis=1).astype(BF16)
+    line = lax.broadcasted_iota(jnp.int32, (16, width), 0)
+    packed = jnp.where(line == 0, g1_ref[...].astype(F32), s1_ref[...].astype(F32))
+    packed = jnp.where(line == 2, g2_ref[...].astype(F32), packed)
+    first_share[section, me, q_part:, :width] = jnp.where(line == 3, s2_ref[...].astype(F32), packed).astype(BF16)
+
     pl.semaphore_wait(barrier, 4)
 
     def weight_copy(model, kind, way):
         owner = chip_peer if way == 2 else me
         target = (
-            lambda: qkv.at[model, owner_rows(owner, q_part), :],
-            lambda: proj.at[model, owner_rows(owner, p_part), :],
-            lambda: expand.at[model, owner_rows(owner * 2, e_part // 2), :],
-            lambda: expand.at[model, owner_rows(owner * 2 + 1, e_part // 2), :],
-            lambda: reduce.at[model, owner_rows(owner * 2, e_part // 2), :],
-            lambda: reduce.at[model, owner_rows(owner * 2 + 1, e_part // 2), :],
-            lambda: norms.at[model],
+            lambda: first_share.at[model, owner],
+            lambda: second_share.at[model, owner],
+            lambda: reduce.at[model, owner_rows(owner, e_part), :],
             lambda: tables.at[model],
         )[kind]()
         device = ({"tp": core_peer}, {"tp": chip_peer}, {"tp": core_peer}, {"section": other})[way]
         return pltpu.make_async_remote_copy(
-            src_ref=table_in if kind == 7 else target, dst_ref=target,
+            src_ref=table_in if kind == 3 else target, dst_ref=target,
             send_sem=w_send.at[model, kind, way], recv_sem=w_recv.at[model, kind, way],
             device_id=device, device_id_type=MESH)
 
@@ -127,6 +128,7 @@
     field_copy = pltpu.make_async_remote_copy(
         src_ref=x_in.at[section], dst_ref=near_raw, send_sem=f_send, recv_sem=f_recv,
         device_id={"lat": pair}, device_id_type=MESH)
+    edges, all_rows = all_edges
     chunks = len(edges) - 1
 
     def pair_copy(part):
@@ -135,11 +137,10 @@
             src_ref=outp.at[0, rows], dst_ref=near_mid.at[rows], send_sem=n_send.at[part],
             recv_sem=n_recv.at[part], device_id={"lat": pair}, device_id_type=MESH)
 
-    def result_copy(model, part):
-        rows = pl.ds(edges[part], edges[part + 1] - edges[part])
+    def result_copy(model):
         return pltpu.make_async_remote_copy(
-            src_ref=outp.at[model, rows], dst_ref=foreign.at[rows], send_sem=o_send.at[part],
-            recv_sem=o_recv.at[part], device_id={"section": other}, device_id_type=MESH)
+            src_ref=outp.at[model], dst_ref=foreign, send_sem=o_send, recv_sem=o_recv,
+            device_id={"section": other}, device_id_type=MESH)
 
     def own_shares(*kinds):
         for kind in kinds:
@@ -148,30 +149,23 @@
         @pl.when(section == 0)
         def _():
             for kind in kinds:
-                if kind < 6:
+                if kind < 3:
                     weight_copy(0, kind, 1).start()
                     weight_copy(0, kind, 0).start()
 
-    own_shares(0, 7)
+    own_shares(0, 3)
     field_copy.start()
-    for load in loads[2:5]:
+    for load in loads[2:8]:
         load.wait()
     tail = lax.broadcasted_iota(jnp.int32, (wide - width, p_part), 0)
     p_tail = jnp.where(
         tail == 0, pb_ref[...].astype(F32), jnp.where(tail == 1, rb_ref[...].astype(F32), 0.0)).T
-    proj[section, owner_rows(me, p_part), :] = jnp.concatenate(
+    second_share[section, me, e_part:, :] = jnp.concatenate(
         [pw_ref[...].astype(F32), p_tail], axis=1).astype(BF16)
-    for load in loads[5:12]:
-        load.wait()
-    line = lax.broadcasted_iota(jnp.int32, (16, width), 0)
-    packed = jnp.where(line == 0, g1_ref[...].astype(F32), s1_ref[...].astype(F32))
-    packed = jnp.where(line == 2, g2_ref[...].astype(F32), packed)
-    norms[section] = jnp.where(line == 3, s2_ref[...].astype(F32), packed).astype(BF16)
-    own_shares(6, 1)
     tail = lax.broadcasted_iota(jnp.int32, (wide - width, e_part), 0)
-    expand[section, owner_rows(me, e_part), :] = jnp.concatenate(
+    second_share[section, me, :e_part, :] = jnp.concatenate(
         [ew_ref[...].astype(F32), jnp.where(tail == 0, eb_ref[...].astype(F32), 0.0)], axis=0).T.astype(BF16)
-    own_shares(2, 3, 4, 5)
+    own_shares(1, 2)
 
     def share_on(kind):
         @pl.when(section == 1)
@@ -230,6 +224,7 @@
         rest = turned - first.astype(F32)
         second = rest.astype(BF16)
         third = (rest - second.astype(F32)).astype(BF16)
+        hand_on(model, 0)
         total = mm(first, pick) + mm(second, pick) + mm(third, pick)
         for wq in range(WW):
             for h in range(heads):
@@ -238,7 +233,6 @@
         bias[...] = spread[...].T * LOG2E
 
     share_on(0)
-    share_on(1)
 
     scale = LOG2E / float(np.sqrt(head_size))
     lane_head = lax.broadcasted_iota(jnp.int32, (half_cells, width), 1)
@@ -247,22 +241,20 @@
     for model in range(2):
         @pl.when(section != model)
         def _():
-            weight_copy(model, 6, 3).wait_recv()
-            weight_copy(model, 7, 3).wait_recv()
+            weight_copy(model, 3, 3).wait_recv()
 
         expand_bias(model)
-        g1, s1, g2, s2 = (norms[model, n:n + 1, :].astype(F32) for n in range(4))
-        hand_on(model, 0)
+        if model == 0:
+            share_on(1)
+        norms = first_share[model, me, q_part:, :width].astype(F32)
+        g1, s1, g2, s2 = (norms[n:n + 1] for n in range(4))
         grid = own_field if model == 0 else outp[0].astype(F32)
         own_n[:, :width] = layer_norm(grid, g1, s1).astype(BF16)
-        if model == 0:
-            share_on(2)
-            share_on(3)
-        hand_on(model, 1)
         weights_here(model, 0)
-        q = mm_nt(own_n[...], qkv[model, :width, :])
-        k_own = mm_nt(own_n[...], qkv[model, width:2 * width, :])
-        v_own = mm_nt(own_n[...], qkv[model, 2 * width:, :])
+        qkv = first_share[model, :, :q_part, :].reshape(3 * width, wide)
+        q = mm_nt(own_n[...], qkv[:width])
+        k_own = mm_nt(own_n[...], qkv[width:2 * width])
+        v_own = mm_nt(own_n[...], qkv[2 * width:])
         if model == 0:
             field_copy.wait_recv()
             near = mm(perm[...], near_raw[...])
@@ -271,11 +263,10 @@
                 pair_copy(part).wait_recv()
             near = near_mid[...].astype(F32)
         near_n[:, :width] = layer_norm(near, g1, s1).astype(BF16)
-        k_near = mm_nt(near_n[...], qkv[model, width:2 * width, :])
-        v_near = mm_nt(near_n[...], qkv[model, 2 * width:, :])
+        k_near = mm_nt(near_n[...], qkv[width:2 * width])
+        v_near = mm_nt(near_n[...], qkv[2 * width:])
         if model == 0:
-            share_on(4)
-            share_on(5)
+            share_on(2)
         attended = []
         for s in range(slabs):
             cut = slice(s * half_cells, (s + 1) * half_cells)
@@ -291,34 +282,33 @@
                 total = jnp.where(m, mixed[h * half_cells:(h + 1) * half_cells], total)
             attended.append(total)
         att_n[:, :width] = jnp.concatenate(attended, axis=0).astype(BF16)
+        hand_on(model, 1)
+        weights_here(model, 1)
+        proj = second_share[model, :, e_part:, :].reshape(width, wide)
+        expand = second_share[model, :, :e_part, :].reshape(tp * e_part, wide)
+        middle = (grid + mm_nt(att_n[...], proj)).astype(BF16).astype(F32)
+        pick_row = (lax.broadcasted_iota(jnp.int32, (16, wide), 1) == width + 1).astype(F32).astype(BF16)
+        shift_out = mm_nt(pick_row, proj)[:1]
+        own_n[:, :width] = layer_norm(middle, g2, s2).astype(BF16)
         hand_on(model, 2)
-        weights_here(model, 1)
-        middle = (grid + mm_nt(att_n[...], proj[model])).astype(BF16).astype(F32)
-        pick_row = (lax.broadcasted_iota(jnp.int32, (16, wide), 1) == width + 1).astype(F32).astype(BF16)
-        shift_out = mm_nt(pick_row, proj[model])[:1]
-        own_n[:, :width] = layer_norm(middle, g2, s2).astype(BF16)
-        for kind in (3, 4, 5):
-            hand_on(model, kind)
         if model == 0:
-            for kind in range(6):
+            for kind in range(3):
                 share_out(1, kind)
-        weights_here(model, 2)
-        weights_here(model, 3)
-        for part in range(chunks):
-            cut = slice(edges[part], edges[part + 1])
-            pre = mm_nt(own_n[cut, :], expand[model])
+        own_edges = all_edges[model]
+        for part in range(len(own_edges) - 1):
+            cut = slice(own_edges[part], own_edges[part + 1])
+            pre = mm_nt(own_n[cut, :], expand)
             hidden = (0.5 * pre * (1.0 + lax.erf(pre * float(np.sqrt(0.5))))).astype(BF16)
             if part == 0:
-                weights_here(model, 4)
-                weights_here(model, 5)
+                weights_here(model, 2)
             result = middle[cut] + shift_out + mm(hidden, reduce[model])
             outp[model, cut, :] = result.astype(BF16)
             if model == 0:
                 pair_copy(part).start()
 
-            @pl.when(section != model)
-            def _():
-                result_copy(model, part).start()
+        @pl.when(section != model)
+        def _():
+            result_copy(model).start()
 
     @pl.when(section == 0)
     def _():
@@ -328,20 +318,19 @@
     def _():
         out_ref[1] = mm(unperm[...], outp[1]).astype(BF16)
 
-    for part in range(chunks):
-        result_copy(other, part).wait_recv()
+    result_copy(other).wait_recv()
     out_ref[other] = mm(unperm[...], foreign[...]).astype(BF16)
 
-    for kind in range(8):
+    for kind in range(4):
         weight_copy(section, kind, 3).wait_send()
     for model in range(2):
-        for kind in range(6):
+        for kind in range(3):
             for way in range(3):
                 weight_copy(model, kind, way).wait_send()
     field_copy.wait_send()
     for part in range(chunks):
         pair_copy(part).wait_send()
-        result_copy(other, part).wait_send()
+    result_copy(other).wait_send()
 
 
 def on_device(
@@ -358,14 +347,14 @@
     wide = -(-(width + 2) // 128) * 128
     lines = -(-heads * GROUP // 8) * 8
     tiles = cells // 16
-    edges = (0, tiles // 2 * 16, (tiles - tiles // 6) * 16, cells)
+    edges = (0, tiles * 2 // 3 * 16, cells)
     chunks = len(edges) - 1
     lanes = -(-WZ * WH * (2 * WW - 1) // 128) * 128
     q_weight, p_weight = qkv_weight[0].T, proj_weight[0].T
     vmem = pl.BlockSpec(memory_space=pltpu.VMEM)
     dma = pltpu.SemaphoreType.DMA
     out = pl.pallas_call(
-        functools.partial(kernel, tp, heads, slabs, edges),
+        functools.partial(kernel, tp, heads, slabs, (edges, (0, cells))),
         out_shape=jax.ShapeDtypeStruct((micro, cells, width), BF16),
         in_specs=[pl.BlockSpec(memory_space=pltpu.HBM)] * 14,
         out_specs=vmem,
@@ -383,11 +372,9 @@
             pltpu.VMEM((1, hidden), BF16),
             pltpu.VMEM(reduce_bias.shape, BF16),
             pltpu.VMEM((2, heads, 1, entries), F32),
-            pltpu.VMEM((2, 3 * width, wide), BF16),
-            pltpu.VMEM((2, width, wide), BF16),
-            pltpu.VMEM((2, tp * hidden, wide), BF16),
+            pltpu.VMEM((2, tp, q_weight.shape[0] + 16, wide), BF16),
+            pltpu.VMEM((2, tp, hidden + p_weight.shape[0], wide), BF16),
             pltpu.VMEM((2, tp * hidden, width), BF16),
-            pltpu.VMEM((2, 16, width), BF16),
             pltpu.VMEM((cells, width), BF16),
             pltpu.VMEM((cells, width), BF16),
             pltpu.VMEM((2, cells, width), BF16),
@@ -401,14 +388,14 @@
             pltpu.VMEM((heads * half_cells, 2 * half_cells), F32),
             pltpu.VMEM((2 * half_cells, heads * half_cells), F32),
             dma((14,)),
-            dma((2, 8, 4)),
-            dma((2, 8, 4)),
+            dma((2, 4, 4)),
+            dma((2, 4, 4)),
             dma,
             dma,
             dma((chunks,)),
             dma((chunks,)),
-            dma((chunks,)),
-            dma((chunks,)),
+            dma,
+            dma,
         ],
         compiler_params=pltpu.CompilerParams(
             collective_id=0, has_side_effects=True, vmem_limit_bytes=60 * 1024 * 1024),

time: 31.9 us -> 31.8 us (level); the launches traced: 31.3 us -> 31.5 us
  no operation moved by 1% of the time
where the time goes in v7:
time: 31.8 us; the launch traced here: 31.5 us
  Pallas kernels  29.8 us (94%)
  local copies, waits for them, and re-layouts  1.69 us (5%)
    pallas_call x1, Pallas kernels, on_device(): pl.pallas_call(functools.partial(kernel, tp, heads, slabs, (edges, (0, ce...  29.8 us
    unnamed x1, local copies, waits for them, and re-layouts  1.69 us

profile of v7, /device:TPU:19, one launch (start us, length us, event | category | flops | bytes accessed | tf_op | source)
XLA Modules:
  0.0 31.5 jit_solution(2025736159589271139)
XLA Ops:
  0.0 29.8 %shard_map.136 = bf16[2,288,192]{2,1,0:T(8,128)(2,1)} custom-call(bf16[2,288,192]{2,1,0:T(8,128)(2,1)} %bitcast.12, bf16[1,192]{1,0:T(2,128)(2,1)} %g1_in.1, bf16[1,192]{1,0:T(2,128)(2,1)} %s1_in.1, bf16[144,192]{1,0:T(8,128)(2,1)} %bitcast.15, bf16[1,144]{1,0:T(2,128)(2,1)} %qb_in.1, bf16[48,192]{1,0:T(8,128)(2,1)} %bitcast.17, bf16[1,48]{1,0:T(2,128)(2,1)} %pb_in.1, ...), custom_call_target="tpu_custom_call" | custom-call | tf_op jit(solution)/shard_map/pallas_call | solution.py:356
  29.8 1.7 %copy.16 = bf16[1,2,2,3,48,192]{5,4,3,2,1,0:T(8,128)(2,1)} copy(bf16[1,2,2,3,48,192]{5,4,3,2,1,0:T(8,128)(2,1)} %bitcast.11) | data formatting | bytes 442368

commit v8 on v5

--- a/solution.py
+++ b/solution.py
@@ -272,6 +272,9 @@
         v_near = mm_nt(near_n[...], qkv[model, 2 * width:, :])
         if model == 0:
             share_on(3)
+        else:
+            hand_on(1, 2)
+            hand_on(1, 3)
         attended = []
         for s in range(slabs):
             cut = slice(s * half_cells, (s + 1) * half_cells)
@@ -286,9 +289,11 @@
             for h, m in enumerate(in_head):
                 total = jnp.where(m, mixed[h * half_cells:(h + 1) * half_cells], total)
             attended.append(total)
+            if model == 0 and s == slabs - 2:
+                hand_on(0, 2)
         att_n[:, :width] = jnp.concatenate(attended, axis=0).astype(BF16)
-        hand_on(model, 2)
-        hand_on(model, 3)
+        if model == 0:
+            hand_on(0, 3)
         weights_here(model, 1)
         middle = (grid + mm_nt(att_n[...], proj[model])).astype(BF16).astype(F32)
         pick_row = (lax.broadcasted_iota(jnp.int32, (16, wide), 1) == width + 1).astype(F32).astype(BF16)

time: 30.9 us -> 31.1 us (level); the launches traced: 30.7 us -> 30.5 us
  no operation moved by 1% of the time
where the time goes in v8:
time: 31.1 us; the launch traced here: 30.5 us
  Pallas kernels  28.8 us (93%)
  local copies, waits for them, and re-layouts  1.69 us (5%)
    pallas_call x1, Pallas kernels, on_device(): pl.pallas_call(functools.partial(kernel, tp, heads, slabs, edges), out_sh...  28.8 us
    unnamed x1, local copies, waits for them, and re-layouts  1.69 us

profile of v8, /device:TPU:19, one launch (start us, length us, event | category | flops | bytes accessed | tf_op | source)
XLA Modules:
  0.0 30.5 jit_solution(8689967102428306847)
XLA Ops:
  0.0 28.8 %shard_map.136 = bf16[2,288,192]{2,1,0:T(8,128)(2,1)} custom-call(bf16[2,288,192]{2,1,0:T(8,128)(2,1)} %bitcast.12, bf16[1,192]{1,0:T(2,128)(2,1)} %g1_in.1, bf16[1,192]{1,0:T(2,128)(2,1)} %s1_in.1, bf16[144,192]{1,0:T(8,128)(2,1)} %bitcast.15, bf16[1,144]{1,0:T(2,128)(2,1)} %qb_in.1, bf16[48,192]{1,0:T(8,128)(2,1)} %bitcast.17, bf16[1,48]{1,0:T(2,128)(2,1)} %pb_in.1, ...), custom_call_target="tpu_custom_call" | custom-call | tf_op jit(solution)/shard_map/pallas_call | solution.py:365
  28.8 1.7 %copy.16 = bf16[1,2,2,3,48,192]{5,4,3,2,1,0:T(8,128)(2,1)} copy(bf16[1,2,2,3,48,192]{5,4,3,2,1,0:T(8,128)(2,1)} %bitcast.11) | data formatting | bytes 442368
